TPU v7x, 32 devices: a whole 2x2x4 slice. The times are simulated.
32 devices in a mesh: dp: 16 (over z, y, core), inner: 2 (over x).
Axes of the slice: x: 2, y: 2, z: 4, core: 2. Of those that a mesh axis runs over, the one named last changes fastest.
Arguments:
- tokens: bfloat16 [16384, 1664], P(('dp', 'inner')), may hold values from -16 to 16
- attn_gain: float32 [1664], replicated, may hold values from 0.1 to 1.9
- qkv_weight: bfloat16 [3, 1664, 832], P(None, 'dp', 'inner'), may hold values from -6 to 6
- out_weight: bfloat16 [832, 1664], P('inner', 'dp'), may hold values from -0.21875 to 0.21875
- merge_gain: float32 [6656], replicated, may hold values from 0.25 to 1.75
- merge_weight: bfloat16 [6656, 2048], P('dp', 'inner'), may hold values from -0.078125 to 0.078125
- segment_ids: int32 [16384], P('dp'), may hold values from -1 to 7, as said below
- owners: int32 [4096, 1], P('dp'), may hold values from 0 to 15; in each aligned block of 256 rows (0 to 255, 256 to 511, ...) at most 32 rows name the same one
Outputs:
- merged_out: bfloat16 [8192, 2048], P('dp', 'inner')
Inputs may be any that keep to these rules, and one draw needn't show every extreme that they name: `segment_ids`: within each device's aligned block of 512 tokens, ids never fall except to -1, which fills a tail of 4 or more tokens; every run of one id starts at a multiple of 4 and holds a multiple of 4 tokens. `owners`: in each aligned block of 256 rows (the rows of one index of dp) no owner is named by more than 32 rows.
All inputs are finite; a program needn't handle non-finite values.
Results may differ from a plain program's by a relative error of at most 0.0062.
Values may be sent and summed in bfloat16 or wider, within the bound.
A program may use at most 128 MiB of HBM per device.

v0:
```python
import jax
import jax.numpy as jnp
from jax import lax
from jax.sharding import PartitionSpec as P

HEAD_DIM = 104


EPS = 1e-06
NEG = -1e30


def layer_norm(values, gain):
    values = values.astype(jnp.float32)
    center = values - jnp.mean(values, axis=-1, keepdims=True)
    spread = jnp.mean(center * center, axis=-1, keepdims=True)
    return center * lax.rsqrt(spread + EPS) * gain


def attend_block(queries, keys, vectors, segment):
    scale = queries.shape[-1] ** (-0.5)
    scores = jnp.einsum("qhe,khe->hqk", queries, keys, preferred_element_type=jnp.float32) * scale
    visible = segment[:, None] == segment[None, :]
    scores = jnp.where(visible[None, :, :], scores, NEG)
    top = jnp.max(scores, axis=-1, keepdims=True)
    weights = jnp.exp(scores - top)
    probs = (weights / jnp.sum(weights, axis=-1, keepdims=True)).astype(jnp.bfloat16)
    context = jnp.einsum("hqk,khe->qhe", probs, vectors, preferred_element_type=jnp.float32)
    return context.astype(jnp.bfloat16)


def split_heads(projected):
    shaped = projected.reshape(3, projected.shape[1], projected.shape[2] // HEAD_DIM, HEAD_DIM)
    return (shaped[0], shaped[1], shaped[2])


def local(tokens, attn_gain, qkv_weight, out_weight, merge_gain, merge_weight, segment_ids, owners):
    tok_rows = tokens.shape[0]
    local_segment = lax.dynamic_slice_in_dim(
        segment_ids, lax.axis_index("inner") * tok_rows, tok_rows
    )
    normed = layer_norm(tokens, attn_gain).astype(jnp.bfloat16)
    qkv_part = lax.all_gather(qkv_weight, "inner", axis=2, tiled=True)
    projected = jnp.einsum(
        "td,cdh->cth",
        normed,
        lax.all_gather(qkv_part, "dp", axis=1, tiled=True),
        preferred_element_type=jnp.float32,
    )
    queries, keys, vectors = split_heads(projected.astype(jnp.bfloat16))
    context = attend_block(queries, keys, vectors, local_segment).reshape(tok_rows, -1)
    out_part = lax.all_gather(out_weight, "inner", axis=0, tiled=True)
    attn_out = jnp.dot(
        context,
        lax.all_gather(out_part, "dp", axis=1, tiled=True),
        preferred_element_type=jnp.float32,
    )
    hidden = tokens.astype(jnp.float32) + attn_out
    quad_rows = hidden.reshape(tok_rows // 4, -1)
    live = local_segment.reshape(-1, 4)[:, 0] >= 0
    merged = jnp.where(live[:, None], layer_norm(quad_rows, merge_gain), 0.0).astype(jnp.bfloat16)
    merge_full = lax.all_gather(merge_weight, "dp", axis=0, tiled=True)
    features = jnp.dot(
        lax.all_gather(merged, "inner", axis=0, tiled=True),
        merge_full,
        preferred_element_type=jnp.float32,
    ).astype(jnp.bfloat16)
    n_dp = lax.axis_size("dp")
    group_rows = features.shape[0]
    slots = 2 * group_rows // n_dp
    owner_col = owners[:, 0]
    chosen = (owner_col[:, None] == jnp.arange(n_dp, dtype=jnp.int32)[None, :]).astype(jnp.int32)
    earlier = jnp.cumsum(chosen, axis=0) - chosen
    rank = jnp.sum(earlier * chosen, axis=1)
    target = owner_col * slots + rank
    source_row = (
        jnp.full((n_dp * slots,), group_rows, jnp.int32)
        .at[target]
        .set(jnp.arange(group_rows, dtype=jnp.int32))
    )
    padded = jnp.concatenate([features, jnp.zeros((1, features.shape[1]), jnp.bfloat16)], axis=0)
    outgoing = padded[source_row]
    return lax.all_to_all(outgoing, "dp", split_axis=0, concat_axis=0, tiled=True)


def solution(mesh):
    placed = (
        P(("dp", "inner"), None),
        P(),
        P(None, "dp", "inner"),
        P("inner", "dp"),
        P(),
        P("dp", "inner"),
        P("dp"),
        P("dp", None),
    )
    return jax.shard_map(
        local, mesh=mesh, in_specs=placed, out_specs=P("dp", "inner"), check_vma=False
    )
```

profile of v0, /device:TPU:0, one launch (start us, length us, event | category | flops | bytes accessed | tf_op | source)
XLA Modules:
  0.0 364.6 jit_solution(17783097113980732867)
XLA Ops:
  6.5 1.4 copy.19
  7.9 13.4 %all_gather.18 = bf16[3,104,832]{1,0,2:T(4,128)(2,1)S(1)} all-gather(bf16[3,104,416]{1,0,2:T(4,128)(2,1)S(1)} %copy.19), channel_id=1, replica_groups=mesh['dp'=16,'inner'=2] {'inner'}, dimensions={2}, use_global_device_ids=true | all-gather | bytes 778752 | tf_op jit(solution)/shard_map/all_gather | solution.py:43
  21.4 1.6 copy.20
  22.9 0.0 all-gather.5.cloned.1.call-update
  22.9 0.0 all-gather.7.cloned.1.call-start
  23.0 5.4 %all_gather.20 = bf16[832,104]{1,0:T(8,128)(2,1)S(1)} all-gather(bf16[416,104]{1,0:T(8,128)(2,1)S(1)} %copy-done.1), channel_id=1, replica_groups=mesh['dp'=16,'inner'=2] {'inner'}, dimensions={0}, use_global_device_ids=true | all-gather | bytes 259584 | tf_op jit(solution)/shard_map/all_gather | solution.py:52
  28.4 0.8 copy.22
  29.2 0.0 all-gather.7.cloned.1.call-update
  29.2 0.0 all-gather.9.cloned.1.call-start
  29.3 0.1 dynamic_slice.3
  29.4 0.1 reshape.93
  29.5 0.1 fusion.19
  29.6 0.3 convert_reduce_fusion
  29.9 0.6 fusion.8
  30.5 0.9 broadcast_compare_fusion
  31.4 71.6 %all-gather.5.cloned.1.call-done = bf16[3,1664,832]{2,1,0:T(8,128)(2,1)} async-done(((bf16[3,104,832]{2,1,0:T(8,128)(2,1)}), bf16[3,1664,832]{2,1,0:T(8,128)(2,1)}) %all-gather.5.cloned.1.call-update) | async-done | bytes 8306704 | tf_op jit(solution)/shard_map/all_gather | solution.py:47
  103.0 11.2 %convert_bitcast_fusion = bf16[3,512,832]{1,2,0:T(8,128)(2,1)S(1)} fusion(bf16[3,1664,832]{2,1,0:T(8,128)(2,1)} %all-gather.5.cloned.1.call-done, bf16[512,1664]{1,0:T(8,128)(2,1)S(1)} %copy-done, f32[1664]{0:T(1024)S(1)} %copy-done.5, f32[512]{0:T(512)S(1)} %add_rsqrt_fusion, f32[512]{0:T(512)S(1)} %broadcast_multiply_fusion), kind=kOutput, calls=%fused_computation.21 | convolution fusion | flops 4258562048 | bytes 12577280 | tf_op jit(solution)/shard_map/td,cdh->cth/dot_general | solution.py:44
  114.3 1.1 fusion.28
  115.3 7.6 %fusion.29 = (f32[8,512]{1,0:T(8,128)S(1)}, f32[8,512,512]{1,2,0:T(8,128)}) fusion(pred[512,512]{0,1:T(8,128)(4,1)} %broadcast_compare_fusion, bf16[512,8,104]{0,2,1:T(8,128)(2,1)} %bitcast.50, bf16[512,8,104]{0,2,1:T(8,128)(2,1)S(1)} %bitcast.49), kind=kOutput, calls=%fused_computation.53 | convolution fusion | flops 444596736 | bytes 10371072 | tf_op jit(solution)/shard_map/sub | solution.py:26
  123.0 4.1 %fusion.16 = bf16[8,104,512]{2,1,0:T(8,128)(2,1)S(1)} fusion(bf16[512,8,104]{0,2,1:T(8,128)(2,1)S(1)} %bitcast.48, f32[8,512,512]{1,2,0:T(8,128)} %get-tuple-element.9, f32[8,512]{1,0:T(8,128)S(1)} %get-tuple-element.8), kind=kOutput, calls=%fused_computation.26 | convolution fusion | flops 440827904 | bytes 10108928 | tf_op jit(solution)/shard_map/hqk,khe->qhe/dot_general | solution.py:28
  127.1 21.2 %all-gather.7.cloned.1.call-done = bf16[832,1664]{0,1:T(8,128)(2,1)} async-done(((bf16[832,104]{0,1:T(8,128)(2,1)}), bf16[832,1664]{0,1:T(8,128)(2,1)}) %all-gather.7.cloned.1.call-update) | async-done | bytes 2768912 | tf_op jit(solution)/shard_map/all_gather | solution.py:55
  148.3 5.7 %fusion.30 = (f32[512]{0:T(512)S(1)}, f32[512,1664]{1,0:T(8,128)}) fusion(bf16[512,832]{0,1:T(8,128)(2,1)S(1)} %bitcast.55, bf16[832,1664]{0,1:T(8,128)(2,1)} %all-gather.7.cloned.1.call-done, bf16[512,1664]{1,0:T(8,128)(2,1)S(1)} %copy-done), kind=kOutput, calls=%fused_computation.54 | convolution fusion | flops 1420230144 | bytes 8734720 | tf_op jit(solution)/shard_map/dot_general | solution.py:53
  154.0 0.1 reduce_sum.74
  154.1 0.1 reduce_sum.75
  154.2 0.1 sub.42
  154.3 0.1 sub.43
  154.4 2.9 reshape.95
  157.4 0.0 copy-start.2
  157.4 2.4 multiply_reduce_fusion
  159.8 0.1 reduce_sum.77
  159.9 0.1 reduce_sum.78
  160.0 0.0 copy-done.2
  160.1 0.0 copy-start.3
  160.1 1.8 select_convert_fusion
  161.9 0.0 all-gather.9.cloned.1.call-update
  161.9 0.0 all-gather.11.cloned.1.call-start
  161.9 0.5 all-gather.11.cloned.1.call-update
  162.5 0.0 copy-done.3
  162.5 0.8 reduce-window.6
  163.3 0.2 slice_reduce_fusion
  163.5 0.1 fusion.22
  163.6 1.4 scatter_custom_fusion
  165.0 43.3 %all-gather.9.cloned.1.call-done = bf16[256,6656]{1,0:T(8,128)(2,1)} async-done(((bf16[128,6656]{1,0:T(8,128)(2,1)}), bf16[256,6656]{1,0:T(8,128)(2,1)}) %all-gather.9.cloned.1.call-update) | async-done | bytes 3407888 | tf_op jit(solution)/shard_map/all_gather | solution.py:64
  208.3 109.5 %all-gather.11.cloned.1.call-done = bf16[6656,1024]{1,0:T(8,128)(2,1)} async-done(((bf16[416,1024]{1,0:T(8,128)(2,1)}), bf16[6656,1024]{1,0:T(8,128)(2,1)}) %all-gather.11.cloned.1.call-update) | async-done | bytes 13631504 | tf_op jit(solution)/shard_map/all_gather | solution.py:62
  317.8 9.6 %convolution_convert_fusion = bf16[256,1024]{1,0:T(8,128)(2,1)S(1)} fusion(bf16[256,6656]{1,0:T(8,128)(2,1)} %all-gather.9.cloned.1.call-done, bf16[6656,1024]{1,0:T(8,128)(2,1)} %all-gather.11.cloned.1.call-done), kind=kOutput, calls=%fused_computation.27 | convolution fusion | flops 3489923072 | bytes 17563648 | tf_op jit(solution)/shard_map/dot_general | solution.py:63
  327.5 2.1 gather_fusion
  329.5 27.5 %all_to_all.12 = bf16[16,32,1024]{2,1,0:T(8,128)(2,1)S(1)} all-to-all(bf16[16,32,1024]{2,1,0:T(8,128)(2,1)S(1)} %bitcast.46), channel_id=1, replica_groups=mesh['dp'=16,'inner'=2] {'dp'}, dimensions={0} | all-to-all | bytes 2097152 | tf_op jit(solution)/shard_map/all_to_all | solution.py:83
  357.1 1.0 copy.28
  (21 shorter events, 0.1 us)
Async XLA Ops:
  6.5 16.5 %copy-start.1 = (bf16[416,104]{1,0:T(8,128)(2,1)S(1)}, bf16[416,104]{1,0:T(8,128)(2,1)}, u32[]{:S(2)}) copy-start(bf16[416,104]{1,0:T(8,128)(2,1)} %param.11) | copy-start | bytes 259588
  6.5 22.7 %copy-start.4 = (s32[1024]{0:T(1024)S(1)}, s32[1024]{0:T(1024)}, u32[]{:S(2)}) copy-start(s32[1024]{0:T(1024)} %param.14) | copy-start | bytes 12292
  6.5 23.1 %copy-start = (bf16[512,1664]{1,0:T(8,128)(2,1)S(1)}, bf16[512,1664]{1,0:T(8,128)(2,1)}, u32[]{:S(2)}) copy-start(bf16[512,1664]{1,0:T(8,128)(2,1)} %param.8) | copy-start | bytes 5111812
  6.5 96.5 %all-gather.5.cloned.1.call-start = ((), (), s32[]{:S(2)}) async-start(), calls=%async_computation.1 | async-start | bytes 9504768 | tf_op jit(solution)/shard_map/all_gather | solution.py:47
  21.4 81.7 %copy-start.5 = (f32[1664]{0:T(1024)S(1)}, f32[1664]{0:T(1024)}, u32[]{:S(2)}) copy-start(f32[1664]{0:T(1024)} %param.9) | copy-start | bytes 19972
  22.9 125.4 %all-gather.7.cloned.1.call-start = ((), (), s32[]{:S(2)}) async-start(), calls=%async_computation.2 | async-start | bytes 3168256 | tf_op jit(solution)/shard_map/all_gather | solution.py:55
  29.2 179.0 %all-gather.9.cloned.1.call-start = ((), (), s32[]{:S(2)}) async-start(), calls=%async_computation.3 | async-start | bytes 5111808 | tf_op jit(solution)/shard_map/all_gather | solution.py:64
  157.4 2.7 copy-start.2
  160.1 2.4 copy-start.3
  161.9 155.9 %all-gather.11.cloned.1.call-start = ((), (), s32[]{:S(2)}) async-start(), calls=%async_computation.4 | async-start | bytes 14483456 | tf_op jit(solution)/shard_map/all_gather | solution.py:62
Sparse Core Ops, SparseCore 0:
  23.1 79.9 all-gather.4
  105.2 43.0 all-gather.6
  162.0 46.2 all-gather.8
  210.4 107.3 all-gather.10
where the time goes:
time: 365 us
  waiting for transfers between devices  246 us (67%)
  blocking collectives  46.3 us (13%)
  matrix products  38.3 us (10%)
  between operations  13.3 us (4%)
  local copies, waits for them, and re-layouts  13 us (4%)
  other arithmetic  7.29 us (2%)
    all_gather x1, waiting for transfers between devices, local(): merge_full = lax.all_gather(merge_weight, 'dp', axis=0, tiled=True)  110 us
    all_gather x1, waiting for transfers between devices, local(): lax.all_gather(qkv_part, 'dp', axis=1, tiled=True)  71.6 us
    all_gather x1, waiting for transfers between devices, local(): lax.all_gather(merged, 'inner', axis=0, tiled=True)  43.3 us
    all_to_all x1, blocking collectives, local(): lax.all_to_all(outgoing, 'dp', split_axis=0, concat_axis=0, tiled=True)  27.5 us
    all_gather x1, waiting for transfers between devices, local(): lax.all_gather(out_part, 'dp', axis=1, tiled=True)  21.2 us
    all_gather x1, blocking collectives, local(): qkv_part = lax.all_gather(qkv_weight, 'inner', axis=2, tiled=True)  13.4 us
    dot_general x1, matrix products, local(): jnp.einsum('td,cdh->cth', normed, lax.all_gather(qkv_part, 'dp', axis=1,...  11.2 us
    dot_general x1, matrix products, local(): jnp.dot(lax.all_gather(merged, 'inner', axis=0, tiled=True), merge_full,...  9.58 us
  transfers between devices with their start and end apart: 4, of which 4 were waited for; matrix products, arithmetic and copies ran while one was open for 8% of the time, Pallas kernels for 0%

commit v1 on v0

--- a/solution.py
+++ b/solution.py
@@ -1,7 +1,13 @@
+import functools
+
 import jax
 import jax.numpy as jnp
 from jax import lax
+from jax.experimental import pallas as pl
+from jax.experimental.pallas import tpu as pltpu
 from jax.sharding import PartitionSpec as P
+
+MESH = pl.DeviceIdType.MESH
 
 HEAD_DIM = 104
 
@@ -83,6 +89,203 @@
     return lax.all_to_all(outgoing, "dp", split_axis=0, concat_axis=0, tiled=True)
 
 
+RING = 8
+
+
+def chip_of(place):
+    place = lax.rem(place + 2 * RING, RING)
+    row = place // 4
+    return 2 * (place + row * (7 - 2 * place)) + row
+
+
+def gather_kernel(sq, so, gq, go, local_sem, send_sem, recv_sem):
+    x = lax.axis_index("inner")
+    dp = lax.axis_index("dp")
+    core = lax.rem(dp, 2)
+    chip = dp // 2
+    z, y = chip // 2, lax.rem(chip, 2)
+    place = z + y * (7 - 2 * z)
+    right = (chip_of(place + 1) * 2 + core, x)
+    left = (chip_of(place - 1) * 2 + core, x)
+    across = (dp, 1 - x)
+    sibling = (chip * 2 + 1 - core, x)
+    mine = 2 * x + core
+    far = 2 * (1 - x) + core
+    split = 112
+
+    barrier = pltpu.get_barrier_semaphore()
+    for other in (right, left, across, sibling):
+        pl.semaphore_signal(barrier, inc=1, device_id=other, device_id_type=MESH)
+    pl.semaphore_wait(barrier, 4)
+
+    pairs = ((sq, gq), (so, go))
+    kept = []
+    for a, (shard, whole) in enumerate(pairs):
+        copy = pltpu.make_async_copy(shard, whole.at[mine, chip], local_sem.at[a])
+        copy.start()
+        kept.append(copy)
+
+    sent = []
+
+    def block(whole, plane, dist, rows):
+        ref = whole.at[plane, chip_of(place + dist)]
+        return ref if rows is None else ref.at[pl.ds(*rows)]
+
+    def send(a, slot, plane, dist, device, rows=None):
+        whole = pairs[a][1]
+        target = block(whole, plane, dist, rows)
+        source = pairs[a][0] if plane is mine and dist == 0 else target
+        if plane is mine and dist == 0 and rows is not None:
+            source = source.at[pl.ds(*rows)]
+        copy = pltpu.make_async_remote_copy(
+            src_ref=source,
+            dst_ref=target,
+            send_sem=send_sem.at[a, slot],
+            recv_sem=recv_sem.at[a, slot],
+            device_id=device,
+            device_id_type=MESH,
+        )
+        copy.start()
+        sent.append(copy)
+
+    def arrived(a, slot, plane, dist, device, rows=None):
+        target = block(pairs[a][1], plane, dist, rows)
+        pltpu.make_async_remote_copy(
+            src_ref=target,
+            dst_ref=target,
+            send_sem=send_sem.at[a, slot],
+            recv_sem=recv_sem.at[a, slot],
+            device_id=device,
+            device_id_type=MESH,
+        ).wait_recv()
+
+    def spread(a, dist):
+        index = dist % RING
+        send(a, 8 + index, mine, dist, across)
+        send(a, 16 + index, mine, dist, sibling)
+
+    top, bottom = (0, split), (split, sq.shape[0] - split)
+    for a in range(2):
+        send(a, 0, mine, 0, right)
+        send(a, 4, mine, 0, left)
+        spread(a, 0)
+    for step in range(1, 4):
+        for a in range(2):
+            arrived(a, step - 1, mine, -step, left)
+            send(a, step, mine, -step, right, top if step == 3 else None)
+            spread(a, -step)
+            arrived(a, 4 + step - 1, mine, step, right)
+            send(a, 4 + step, mine, step, left, bottom if step == 3 else None)
+            spread(a, step)
+    for a in range(2):
+        arrived(a, 3, mine, 4, left, top)
+        arrived(a, 7, mine, 4, right, bottom)
+        spread(a, 4)
+    order = (0, -1, 1, -2, 2, -3, 3, 4)
+    for dist in order:
+        for a in range(2):
+            arrived(a, 8 + dist % RING, far, dist, across)
+            send(a, 24 + dist % RING, far, dist, sibling)
+    near_other = 2 * x + 1 - core
+    far_other = 2 * (1 - x) + 1 - core
+    for dist in order:
+        for a in range(2):
+            arrived(a, 16 + dist % RING, near_other, dist, sibling)
+            arrived(a, 24 + dist % RING, far_other, dist, sibling)
+    for copy in sent:
+        copy.wait_send()
+    for copy in kept:
+        copy.wait()
+
+
+def gather_heads(sq, so):
+    return pl.pallas_call(
+        gather_kernel,
+        out_shape=(
+            jax.ShapeDtypeStruct((4, RING) + sq.shape, sq.dtype),
+            jax.ShapeDtypeStruct((4, RING) + so.shape, so.dtype),
+        ),
+        in_specs=[pl.BlockSpec(memory_space=pl.ANY)] * 2,
+        out_specs=(pl.BlockSpec(memory_space=pl.ANY),) * 2,
+        scratch_shapes=[
+            pltpu.SemaphoreType.DMA((2,)),
+            pltpu.SemaphoreType.DMA((2, 32)),
+            pltpu.SemaphoreType.DMA((2, 32)),
+        ],
+        compiler_params=pltpu.CompilerParams(collective_id=0, has_side_effects=True),
+        cost_estimate=pl.CostEstimate(flops=0, bytes_accessed=200_000_000, transcendentals=0),
+    )(sq, so)
+
+
+def pair_shards(qkv_weight, out_weight):
+    depth = qkv_weight.shape[1]
+    half = qkv_weight.shape[2] // 2
+    core = lax.rem(lax.axis_index("dp"), 2)
+    heads = qkv_weight.reshape(3, depth, 2, half).transpose(2, 1, 0, 3).reshape(2, depth, 3 * half)
+    outs = out_weight.reshape(2, half, depth).transpose(0, 2, 1)
+    both = jnp.concatenate([heads, outs], axis=2)
+    keep = jnp.where(core == 0, both[0], both[1])
+    give = jnp.where(core == 0, both[1], both[0])
+    n_dp = lax.axis_size("dp")
+    got = lax.ppermute(give, "dp", [(i, i ^ 1) for i in range(n_dp)])
+    shard = jnp.concatenate(
+        [jnp.where(core == 0, keep, got), jnp.where(core == 0, got, keep)], axis=0
+    )
+    return shard[:, : 3 * half], shard[:, 3 * half :]
+
+
+def attend_pairs(projected, segment):
+    pairs, rows, width = projected.shape
+    shaped = projected.reshape(pairs, rows, 3, 2, HEAD_DIM)
+    queries, keys, vectors = shaped[:, :, 0], shaped[:, :, 1], shaped[:, :, 2]
+    scale = HEAD_DIM ** (-0.5)
+    scores = jnp.einsum("pqhe,pkhe->phqk", queries, keys, preferred_element_type=jnp.float32) * scale
+    visible = segment[:, None] == segment[None, :]
+    scores = jnp.where(visible[None, None], scores, NEG)
+    top = jnp.max(scores, axis=-1, keepdims=True)
+    weights = jnp.exp(scores - top)
+    probs = (weights / jnp.sum(weights, axis=-1, keepdims=True)).astype(jnp.bfloat16)
+    context = jnp.einsum("phqk,pkhe->pqhe", probs, vectors, preferred_element_type=jnp.float32)
+    return context.astype(jnp.bfloat16).reshape(pairs, rows, 2 * HEAD_DIM)
+
+
+def local_ring(tokens, attn_gain, qkv_weight, out_weight, merge_gain, merge_weight, segment_ids, owners):
+    tok_rows, width = tokens.shape
+    local_segment = lax.dynamic_slice_in_dim(
+        segment_ids, lax.axis_index("inner") * tok_rows, tok_rows
+    )
+    merge_full = lax.all_gather(merge_weight, "dp", axis=0, tiled=True)
+    sq, so = pair_shards(qkv_weight, out_weight)
+    gq, go = gather_heads(sq, so)
+    gq = gq.reshape(4, width, sq.shape[1])
+    go = go.reshape(4, width, so.shape[1])
+    normed = layer_norm(tokens, attn_gain).astype(jnp.bfloat16)
+    projected = jnp.einsum("td,pdn->ptn", normed, gq, preferred_element_type=jnp.float32)
+    context = attend_pairs(projected.astype(jnp.bfloat16), local_segment)
+    attn_out = jnp.einsum("ptn,pdn->td", context, go, preferred_element_type=jnp.float32)
+    hidden = tokens.astype(jnp.float32) + attn_out
+    quad_rows = hidden.reshape(tok_rows // 4, -1)
+    live = local_segment.reshape(-1, 4)[:, 0] >= 0
+    merged = jnp.where(live[:, None], layer_norm(quad_rows, merge_gain), 0.0).astype(jnp.bfloat16)
+    theirs = lax.ppermute(merged, "inner", [(0, 1), (1, 0)])
+    first = lax.axis_index("inner") == 0
+    group = jnp.concatenate(
+        [jnp.where(first, merged, theirs), jnp.where(first, theirs, merged)], axis=0
+    )
+    features = jnp.dot(group, merge_full, preferred_element_type=jnp.float32).astype(jnp.bfloat16)
+    n_dp = lax.axis_size("dp")
+    group_rows = features.shape[0]
+    slots = 2 * group_rows // n_dp
+    owner_col = owners[:, 0]
+    chosen = (owner_col[:, None] == jnp.arange(n_dp, dtype=jnp.int32)[None, :]).astype(jnp.int32)
+    earlier = jnp.cumsum(chosen, axis=0) - chosen
+    rank = jnp.sum(earlier * chosen, axis=1)
+    target = owner_col * slots + rank
+    place = (jnp.arange(n_dp * slots, dtype=jnp.int32)[:, None] == target[None, :]).astype(jnp.bfloat16)
+    outgoing = jnp.dot(place, features, preferred_element_type=jnp.float32).astype(jnp.bfloat16)
+    return lax.all_to_all(outgoing, "dp", split_axis=0, concat_axis=0, tiled=True)
+
+
 def solution(mesh):
     placed = (
         P(("dp", "inner"), None),
@@ -94,6 +297,7 @@
         P("dp"),
         P("dp", None),
     )
+    ringed = dict(mesh.shape) == {"dp": 16, "inner": 2}
     return jax.shard_map(
-        local, mesh=mesh, in_specs=placed, out_specs=P("dp", "inner"), check_vma=False
-    )
+        local_ring if ringed else local, mesh=mesh, in_specs=placed, out_specs=P("dp", "inner"), check_vma=False
+    )

time: 365 us -> 221 us (0.61)
  waiting for transfers between devices: 246 us -> 38.9 us
  Pallas kernels: 0 us -> 77.8 us
  blocking collectives: 46.3 us -> 33.8 us
  other arithmetic: 7.29 us -> 18.3 us
  matrix products: 38.3 us -> 28.5 us
  local copies, waits for them, and re-layouts: 13 us -> 8.05 us
    all_gather x4 -> x1, waiting for transfers between devices: 246 us -> 0.01 us  [local_ring(): merge_full = lax.all_gather(merge_weight, 'dp', axis=0, tiled=True)]
    pallas_call x0 -> x1, Pallas kernels: none -> 77.8 us  [gather_heads(): pl.pallas_call(gather_kernel, out_shape=(jax.ShapeDtypeStruct((4, RING) +...]
    ppermute x0 -> x2, waiting for transfers between devices: none -> 38.2 us  [the longest x1 38.2 us: local_ring(): theirs = lax.ppermute(merged, 'inner', [(0, 1), (1, 0)])]
    all_gather x2 -> x0, blocking collectives: 18.8 us -> none  [the longest x1 13.4 us: local(): qkv_part = lax.all_gather(qkv_weight, 'inner', axis=2, tiled=True)]
    sub x1 -> x0, matrix products: 7.65 us -> none  [attend_block(): weights = jnp.exp(scores - top)]
    all_to_all x1, blocking collectives: 27.5 us -> 33.8 us  [local_ring(): lax.all_to_all(outgoing, 'dp', split_axis=0, concat_axis=0, tiled=True)]
    sub x0 -> x1, other arithmetic: none -> 5.67 us  [attend_pairs(): weights = jnp.exp(scores - top)]
    select_n x2 -> x3, other arithmetic: 0.01 us -> 4.57 us  [the longest x1 4.28 us: local_ring(): jnp.where(first, merged, theirs)]
  transfers between devices with their start and end apart: 4 -> 3, of which waited for: 4 -> 1; matrix products, arithmetic and copies ran while one was open for 8% -> 20% of each run, Pallas kernels for 0% -> 35%
where the time goes in v1:
time: 221 us; the launch traced here: 220 us
  Pallas kernels  77.8 us (35%)
  waiting for transfers between devices  38.9 us (18%)
  blocking collectives  33.8 us (15%)
  matrix products  28.5 us (13%)
  other arithmetic  18.3 us (8%)
  between operations  13.6 us (6%)
  local copies, waits for them, and re-layouts  8.05 us (4%)
    pallas_call x1, Pallas kernels, gather_heads(): pl.pallas_call(gather_kernel, out_shape=(jax.ShapeDtypeStruct((4, RING) +...  77.8 us
    ppermute x1, waiting for transfers between devices, local_ring(): theirs = lax.ppermute(merged, 'inner', [(0, 1), (1, 0)])  38.2 us
    all_to_all x1, blocking collectives, local_ring(): lax.all_to_all(outgoing, 'dp', split_axis=0, concat_axis=0, tiled=True)  33.8 us
    dot_general x1, matrix products, local_ring(): jnp.dot(place, features, preferred_element_type=jnp.float32)  9.86 us
    dot_general x1, matrix products, local_ring(): jnp.einsum('td,pdn->ptn', normed, gq, preferred_element_type=jnp.float32)  9.03 us
    sub x1, other arithmetic, attend_pairs(): weights = jnp.exp(scores - top)  5.67 us
  transfers between devices with their start and end apart: 3, of which 1 were waited for; matrix products, arithmetic and copies ran while one was open for 20% of the time, Pallas kernels for 35%

profile of v1, /device:TPU:0, one launch (start us, length us, event | category | flops | bytes accessed | tf_op | source)
XLA Modules:
  0.0 220.1 jit_solution(4952444771403077564)
XLA Ops:
  6.5 0.0 all-gather.2.cloned.1.call-start
  6.5 0.7 all-gather.2.cloned.1.call-update
  7.3 1.2 reshape.117
  8.5 0.7 copy.27
  9.2 0.2 copy.29
  9.4 1.0 copy.28
  10.4 0.0 copy-start.5
  10.4 0.1 select_bitcast_fusion
  10.5 0.5 collective-permute-start
  11.0 0.0 copy-done.3
  11.0 0.1 dynamic_slice.3
  11.1 0.1 reshape.116
  11.2 0.1 fusion.30
  11.3 0.0 copy-done
  11.3 0.3 convert_reduce_fusion
  11.6 0.2 broadcast_compare_fusion
  11.9 0.6 fusion.8
  12.5 0.0 collective-permute-done
  12.5 0.2 bitcast_select_fusion
  12.7 0.7 pad_maximum_fusion.1.so
  13.4 0.7 fusion.27.sq
  14.1 77.8 %shard_map.82 = (bf16[4,8,208,624]{3,2,1,0:T(8,128)(2,1)}, bf16[4,8,208,208]{3,2,1,0:T(8,128)(2,1)}) custom-call(bf16[208,624]{1,0:T(8,128)(2,1)} %fusion.27.sq, bf16[208,208]{1,0:T(8,128)(2,1)} %pad_maximum_fusion.1.so), custom_call_target="tpu_custom_call" | custom-call | bytes 200000000 | tf_op jit(solution)/shard_map/pallas_call | solution.py:202
  91.9 0.0 copy-done.5
  91.9 9.0 %convolution_convert_fusion = bf16[4,624,512]{2,1,0:T(8,128)(2,1)S(1)} fusion(bf16[4,1664,624]{2,1,0:T(8,128)(2,1)} %bitcast.76, bf16[512,1664]{1,0:T(8,128)(2,1)S(1)} %copy-done, f32[1664]{0:T(1024)S(1)} %copy-done.5, f32[512]{0:T(512)S(1)} %add_rsqrt_fusion, f32[512]{0:T(512)S(1)} %broadcast_multiply_fusion), kind=kOutput, calls=%fused_computation.23 | convolution fusion | flops 4258562048 | bytes 12577280 | tf_op jit(solution)/shard_map/td,pdn->ptn/dot_general | solution.py:263
  100.9 1.3 fusion.26
  102.2 5.7 %fusion.39 = (f32[4,2,512]{2,1,0:T(2,128)S(1)}, f32[4,2,512,512]{2,3,1,0:T(8,128)}) fusion(f32[4,2,512,512]{2,3,1,0:T(8,128)S(1)} %fusion.26, pred[512,512]{0,1:T(8,128)(4,1)S(1)} %broadcast_compare_fusion), kind=kOutput, calls=%fused_computation.71 | output fusion | flops 12583423 | bytes 17055744 | tf_op jit(solution)/shard_map/sub | solution.py:246
  107.9 4.4 %fusion.20 = bf16[4,2,104,512]{3,2,1,0:T(8,128)(2,1)S(1)} fusion(f32[4,2,512,512]{2,3,1,0:T(8,128)} %get-tuple-element.14, f32[4,2,512]{2,1,0:T(2,128)S(1)} %get-tuple-element.13, bf16[4,512,3,2,104]{1,4,3,2,0:T(8,128)(2,1)S(1)} %bitcast.67), kind=kOutput, calls=%fused_computation.31 | convolution fusion | flops 440827904 | bytes 10108928 | tf_op jit(solution)/shard_map/phqk,pkhe->pqhe/dot_general | solution.py:248
  112.3 0.1 copy-done.4
  112.4 3.9 %fusion.40 = (f32[512]{0:T(512)S(1)}, f32[512,1664]{1,0:T(8,128)}) fusion(bf16[4,512,208]{1,2,0:T(8,128)(2,1)S(1)} %bitcast.78, bf16[4,1664,208]{2,1,0:T(8,128)(2,1)S(1)} %bitcast.77, bf16[512,1664]{1,0:T(8,128)(2,1)S(1)} %copy-done), kind=kOutput, calls=%fused_computation.72 | convolution fusion | flops 1420230144 | bytes 8734720 | tf_op jit(solution)/shard_map/ptn,pdn->td/dot_general | solution.py:265
  116.3 0.1 reduce_sum.73
  116.4 0.1 reduce_sum.74
  116.5 0.1 sub.43
  116.6 0.1 sub.44
  116.7 3.1 %reshape.124 = f32[128,6656]{1,0:T(8,128)S(1)} reshape(f32[512,1664]{1,0:T(8,128)} %get-tuple-element.16) | data formatting | bytes 6815744 | tf_op jit(solution)/shard_map/reshape | solution.py:267
  119.9 0.0 copy-start.1
  119.9 2.6 %multiply_reduce_fusion = f32[512]{0:T(512)S(1)} fusion(f32[512,1664]{1,0:T(8,128)} %get-tuple-element.16, f32[512]{0:T(512)S(1)} %sub.44), kind=kLoop, calls=%fused_computation.22 | loop fusion | flops 2555392 | bytes 3411968 | tf_op jit(solution)/shard_map/reduce_sum | solution.py:22
  122.5 0.1 reduce_sum.76
  122.6 0.1 reduce_sum.77
  122.8 1.8 select_convert_fusion
  124.5 0.6 collective-permute-start.1
  125.1 0.6 reduce-window.6
  125.7 0.2 slice_reduce_fusion
  126.0 0.1 fusion.33
  126.1 38.2 %collective-permute-done.1 = bf16[128,6656]{1,0:T(8,128)(2,1)} collective-permute-done((bf16[128,6656]{1,0:T(8,128)(2,1)}, bf16[128,6656]{1,0:T(8,128)(2,1)}, u32[]{:S(2)}, u32[]{:S(2)}) %collective-permute-start.1) | collective-permute-done | bytes 1703968 | tf_op jit(solution)/shard_map/ppermute | solution.py:270
  164.3 4.3 %broadcast_select_fusion.1 = (bf16[128,6656]{1,0:T(8,128)(2,1)}, bf16[128,6656]{1,0:T(8,128)(2,1)}) fusion(bf16[128,6656]{1,0:T(8,128)(2,1)} %collective-permute-done.1, pred[]{:T(512)S(6)} %eq.72, f32[6656]{0:T(1024)S(1)} %copy-done.1, f32[128]{0:T(128)S(1)} %add_rsqrt_fusion.1, f32[128,6656]{1,0:T(8,128)S(1)} %reshape.124, ...), kind=kLoop, calls=%fused_computation.29 | loop fusion | flops 5963776 | bytes 8547457 | tf_op jit(solution)/shard_map/jit(_where)/select_n | solution.py:273
  168.5 9.9 %convolution_convert_fusion.1 = bf16[512,1024]{1,0:T(8,128)(2,1)S(1)} fusion(bf16[6656,1024]{1,0:T(8,128)(2,1)} %all-gather.2.cloned.1.call-done, bf16[128,6656]{1,0:T(8,128)(2,1)} %get-tuple-element.10, bf16[128,6656]{1,0:T(8,128)(2,1)} %get-tuple-element.9, s32[256]{0:T(256)S(1)} %multiply_add_fusion), kind=kOutput, calls=%fused_computation.30 | convolution fusion | flops 3765829632 | bytes 18088960 | tf_op jit(solution)/shard_map/dot_general | solution.py:285
  178.4 33.8 %all_to_all.12 = bf16[16,32,1024]{2,1,0:T(8,128)(2,1)S(1)} all-to-all(bf16[16,32,1024]{2,1,0:T(8,128)(2,1)S(1)} %bitcast.69), channel_id=1, replica_groups=mesh['dp'=16,'inner'=2] {'dp'}, dimensions={0} | all-to-all | bytes 2097152 | tf_op jit(solution)/shard_map/all_to_all | solution.py:286
  212.3 1.0 copy.45
  (15 shorter events, 0.1 us)
Async XLA Ops:
  6.5 4.5 %copy-start.3 = (s32[1024]{0:T(1024)S(1)}, s32[1024]{0:T(1024)}, u32[]{:S(2)}) copy-start(s32[1024]{0:T(1024)} %param.14) | copy-start | bytes 12292
  6.5 4.8 %copy-start = (bf16[512,1664]{1,0:T(8,128)(2,1)S(1)}, bf16[512,1664]{1,0:T(8,128)(2,1)}, u32[]{:S(2)}) copy-start(bf16[512,1664]{1,0:T(8,128)(2,1)} %param.8) | copy-start | bytes 5111812
  6.5 162.0 %all-gather.2.cloned.1.call-start = ((), (), s32[]{:S(2)}) async-start(), calls=%async_computation.1 | async-start | bytes 14483456 | tf_op jit(solution)/shard_map/all_gather | solution.py:257
  10.4 81.5 %copy-start.5 = (f32[1664]{0:T(1024)S(1)}, f32[1664]{0:T(1024)}, u32[]{:S(2)}) copy-start(f32[1664]{0:T(1024)} %param.9) | copy-start | bytes 19972
  10.5 2.0 collective-permute-start
  107.9 4.5 %copy-start.4 = (bf16[4,8,208,208]{3,2,1,0:T(8,128)(2,1)S(1)}, bf16[4,8,208,208]{3,2,1,0:T(8,128)(2,1)}, u32[]{:S(2)}) copy-start(bf16[4,8,208,208]{3,2,1,0:T(8,128)(2,1)} %get-tuple-element.8) | copy-start | bytes 8306692
  119.9 2.9 %copy-start.1 = (f32[6656]{0:T(1024)S(1)}, f32[6656]{0:T(1024)}, u32[]{:S(2)}) copy-start(f32[6656]{0:T(1024)} %param.12) | copy-start | bytes 79876
  122.5 2.6 %copy-start.2 = (s32[256,1]{0,1:T(1,128)S(1)}, s32[256,1]{0,1:T(1,128)}, u32[]{:S(2)}) copy-start(s32[256,1]{0,1:T(1,128)} %param.15) | copy-start | bytes 3076
  124.5 39.7 %collective-permute-start.1 = (bf16[128,6656]{1,0:T(8,128)(2,1)}, bf16[128,6656]{1,0:T(8,128)(2,1)}, u32[]{:S(2)}, u32[]{:S(2)}) collective-permute-start(bf16[128,6656]{1,0:T(8,128)(2,1)} %select_convert_fusion), channel_id=1, source_target_pairs={{0,1},{1,0},{2,3},{3,2},{4,5},{5,4},{6,7},{7,6},{8,9},{9,8},{10,11... | collective-permute-start | bytes 5111816 | tf_op jit(solution)/shard_map/ppermute | solution.py:270
Sparse Core Ops, SparseCore 0:
  9.7 133.3 all-gather.1

commit v2 on v1

--- a/solution.py
+++ b/solution.py
@@ -217,6 +217,113 @@
     )(sq, so)
 
 
+TAIL_COLS = 256
+
+
+def tail_kernel(own, theirs, weight, place, out, rows, wide, feat, load_sem, keep_sem, send_sem, recv_sem):
+    x = lax.axis_index("inner")
+    me = lax.axis_index("dp")
+    peers = lax.axis_size("dp")
+    half = own.shape[0]
+    slots = out.shape[0] // peers
+    chunks = weight.shape[1] // TAIL_COLS
+
+    loads = [
+        pltpu.make_async_copy(own, rows.at[pl.ds(0, half)], load_sem.at[chunks]),
+        pltpu.make_async_copy(theirs, rows.at[pl.ds(half, half)], load_sem.at[chunks + 1]),
+    ]
+    for chunk in range(chunks):
+        loads.append(
+            pltpu.make_async_copy(
+                weight.at[:, pl.ds(chunk * TAIL_COLS, TAIL_COLS)], wide.at[chunk], load_sem.at[chunk]
+            )
+        )
+    for load in loads:
+        load.start()
+
+    barrier = pltpu.get_barrier_semaphore()
+    for step in range(1, peers):
+        other = lax.rem(me + step, peers)
+        pl.semaphore_signal(barrier, inc=1, device_id=(other, x), device_id_type=MESH)
+    loads[0].wait()
+    loads[1].wait()
+
+    copies = []
+    for chunk in range(chunks):
+        loads[2 + chunk].wait()
+        product = jnp.dot(rows[...], wide[chunk], preferred_element_type=jnp.float32)
+        feat[chunk] = jnp.dot(
+            place[...], product.astype(jnp.bfloat16), preferred_element_type=jnp.float32
+        ).astype(jnp.bfloat16)
+        if chunk == 0:
+            pl.semaphore_wait(barrier, peers - 1)
+        columns = pl.ds(chunk * TAIL_COLS, TAIL_COLS)
+        landing = out.at[pl.ds(pl.multiple_of(me * slots, slots), slots), columns]
+        for step in range(1, peers):
+            other = lax.rem(me + step, peers)
+            copy = pltpu.make_async_remote_copy(
+                src_ref=feat.at[chunk, pl.ds(pl.multiple_of(other * slots, slots), slots)],
+                dst_ref=landing,
+                send_sem=send_sem.at[chunk, step],
+                recv_sem=recv_sem.at[chunk, step],
+                device_id=(other, x),
+                device_id_type=MESH,
+            )
+            copy.start()
+            copies.append(copy)
+        keep = pltpu.make_async_copy(
+            feat.at[chunk, pl.ds(pl.multiple_of(me * slots, slots), slots)], landing, keep_sem.at[chunk]
+        )
+        keep.start()
+        copies.append(keep)
+    for chunk in range(chunks):
+        columns = pl.ds(chunk * TAIL_COLS, TAIL_COLS)
+        for step in range(1, peers):
+            giver = lax.rem(me + peers - step, peers)
+            landing = out.at[pl.ds(pl.multiple_of(giver * slots, slots), slots), columns]
+            pltpu.make_async_remote_copy(
+                src_ref=landing,
+                dst_ref=landing,
+                send_sem=send_sem.at[chunk, step],
+                recv_sem=recv_sem.at[chunk, step],
+                device_id=(giver, x),
+                device_id_type=MESH,
+            ).wait_recv()
+    for number, copy in enumerate(copies):
+        if number % peers == peers - 1:
+            copy.wait()
+        else:
+            copy.wait_send()
+
+
+def merge_and_route(own, theirs, weight, place):
+    peers = lax.axis_size("dp")
+    out_rows, group = place.shape
+    depth, columns = weight.shape
+    chunks = columns // TAIL_COLS
+    return pl.pallas_call(
+        tail_kernel,
+        out_shape=jax.ShapeDtypeStruct((out_rows, columns), jnp.bfloat16),
+        in_specs=[pl.BlockSpec(memory_space=pl.ANY)] * 3 + [pl.BlockSpec(memory_space=pltpu.VMEM)],
+        out_specs=pl.BlockSpec(memory_space=pl.ANY),
+        scratch_shapes=[
+            pltpu.VMEM((group, depth), jnp.bfloat16),
+            pltpu.VMEM((chunks, depth, TAIL_COLS), jnp.bfloat16),
+            pltpu.VMEM((chunks, out_rows, TAIL_COLS), jnp.bfloat16),
+            pltpu.SemaphoreType.DMA((chunks + 2,)),
+            pltpu.SemaphoreType.DMA((chunks,)),
+            pltpu.SemaphoreType.DMA((chunks, peers)),
+            pltpu.SemaphoreType.DMA((chunks, peers)),
+        ],
+        compiler_params=pltpu.CompilerParams(
+            collective_id=1, has_side_effects=True, vmem_limit_bytes=56 * 1024 * 1024
+        ),
+        cost_estimate=pl.CostEstimate(
+            flops=2 * group * depth * columns, bytes_accessed=2 * depth * columns, transcendentals=0
+        ),
+    )(own, theirs, weight, place)
+
+
 def pair_shards(qkv_weight, out_weight):
     depth = qkv_weight.shape[1]
     half = qkv_weight.shape[2] // 2
@@ -268,22 +375,21 @@
     live = local_segment.reshape(-1, 4)[:, 0] >= 0
     merged = jnp.where(live[:, None], layer_norm(quad_rows, merge_gain), 0.0).astype(jnp.bfloat16)
     theirs = lax.ppermute(merged, "inner", [(0, 1), (1, 0)])
-    first = lax.axis_index("inner") == 0
-    group = jnp.concatenate(
-        [jnp.where(first, merged, theirs), jnp.where(first, theirs, merged)], axis=0
-    )
-    features = jnp.dot(group, merge_full, preferred_element_type=jnp.float32).astype(jnp.bfloat16)
     n_dp = lax.axis_size("dp")
-    group_rows = features.shape[0]
-    slots = 2 * group_rows // n_dp
+    half_rows = merged.shape[0]
+    slots = 4 * half_rows // n_dp
     owner_col = owners[:, 0]
     chosen = (owner_col[:, None] == jnp.arange(n_dp, dtype=jnp.int32)[None, :]).astype(jnp.int32)
     earlier = jnp.cumsum(chosen, axis=0) - chosen
     rank = jnp.sum(earlier * chosen, axis=1)
     target = owner_col * slots + rank
+    target = jnp.where(
+        lax.axis_index("inner") == 0,
+        target,
+        jnp.concatenate([target[half_rows:], target[:half_rows]]),
+    )
     place = (jnp.arange(n_dp * slots, dtype=jnp.int32)[:, None] == target[None, :]).astype(jnp.bfloat16)
-    outgoing = jnp.dot(place, features, preferred_element_type=jnp.float32).astype(jnp.bfloat16)
-    return lax.all_to_all(outgoing, "dp", split_axis=0, concat_axis=0, tiled=True)
+    return merge_and_route(merged, theirs, merge_full, place)
 
 
 def solution(mesh):

time: 221 us -> 208 us (0.941)
  blocking collectives: 33.8 us -> 0 us
  Pallas kernels: 77.8 us -> 111 us
  matrix products: 28.5 us -> 18.6 us
  other arithmetic: 18.3 us -> 14.8 us
  local copies, waits for them, and re-layouts: 8.05 us -> 10.5 us
    all_to_all x1 -> x0, blocking collectives: 33.8 us -> none  [local_ring(): lax.all_to_all(outgoing, 'dp', split_axis=0, concat_axis=0, tiled=True)]
    pallas_call x0 -> x1, Pallas kernels: none -> 33.4 us  [merge_and_route(): pl.pallas_call(tail_kernel, out_shape=jax.ShapeDtypeStruct((out_rows, col...]
    dot_general x1 -> x0, matrix products: 9.86 us -> none  [local_ring(): jnp.dot(place, features, preferred_element_type=jnp.float32)]
    select_n x1, other arithmetic: 4.28 us -> 0.01 us  [local_ring(): jnp.where(lax.axis_index('inner') == 0, target, jnp.concatenate([target[h...]
    unnamed x13 -> x15, local copies, waits for them, and re-layouts: 1.09 us -> 3.56 us
  transfers between devices with their start and end apart: 3 -> 3, of which waited for: 1 -> 1; matrix products, arithmetic and copies ran while one was open for 20% -> 19% of each run, Pallas kernels for 35% -> 37%
where the time goes in v2:
time: 208 us
  Pallas kernels  111 us (53%)
  waiting for transfers between devices  38 us (18%)
  matrix products  18.6 us (9%)
  other arithmetic  14.8 us (7%)
  between operations  13.6 us (7%)
  local copies, waits for them, and re-layouts  10.5 us (5%)
    pallas_call x1, Pallas kernels, gather_heads(): pl.pallas_call(gather_kernel, out_shape=(jax.ShapeDtypeStruct((4, RING) +...  77.8 us
    ppermute x1, waiting for transfers between devices, local_ring(): theirs = lax.ppermute(merged, 'inner', [(0, 1), (1, 0)])  37.3 us
    pallas_call x1, Pallas kernels, merge_and_route(): pl.pallas_call(tail_kernel, out_shape=jax.ShapeDtypeStruct((out_rows, col...  33.4 us
    dot_general x1, matrix products, local_ring(): jnp.einsum('td,pdn->ptn', normed, gq, preferred_element_type=jnp.float32)  9.03 us
    sub x1, other arithmetic, attend_pairs(): weights = jnp.exp(scores - top)  5.67 us
    dot_general x1, matrix products, attend_pairs(): jnp.einsum('phqk,pkhe->pqhe', probs, vectors, preferred_element_type=jnp....  4.38 us
  transfers between devices with their start and end apart: 3, of which 1 were waited for; matrix products, arithmetic and copies ran while one was open for 19% of the time, Pallas kernels for 37%

profile of v2, /device:TPU:0, one launch (start us, length us, event | category | flops | bytes accessed | tf_op | source)
XLA Modules:
  0.0 207.9 jit_solution(14528268374266524899)
XLA Ops:
  6.5 0.0 all-gather.2.cloned.1.call-start
  6.5 0.7 all-gather.2.cloned.1.call-update
  7.3 1.2 reshape.129
  8.5 0.7 copy.26
  9.2 0.2 copy.28
  9.4 1.0 copy.27
  10.4 0.0 copy-start.6
  10.4 0.1 select_bitcast_fusion
  10.5 0.5 collective-permute-start
  11.0 0.0 copy-done.4
  11.0 0.1 dynamic_slice.3
  11.1 0.1 reshape.128
  11.2 0.1 fusion.21
  11.3 0.0 copy-done
  11.3 0.3 convert_reduce_fusion
  11.6 0.2 broadcast_compare_fusion
  11.9 0.6 fusion.8
  12.5 0.0 collective-permute-done
  12.5 0.2 bitcast_select_fusion
  12.7 0.7 pad_maximum_fusion.1.so
  13.4 0.7 fusion.19.sq
  14.1 77.8 %shard_map.82 = (bf16[4,8,208,624]{3,2,1,0:T(8,128)(2,1)}, bf16[4,8,208,208]{3,2,1,0:T(8,128)(2,1)}) custom-call(bf16[208,624]{1,0:T(8,128)(2,1)} %fusion.19.sq, bf16[208,208]{1,0:T(8,128)(2,1)} %pad_maximum_fusion.1.so), custom_call_target="tpu_custom_call" | custom-call | bytes 200000000 | tf_op jit(solution)/shard_map/pallas_call | solution.py:202
  91.9 0.0 copy-done.6
  91.9 9.0 %convolution_convert_fusion = bf16[4,624,512]{2,1,0:T(8,128)(2,1)S(1)} fusion(bf16[4,1664,624]{2,1,0:T(8,128)(2,1)} %bitcast.71, bf16[512,1664]{1,0:T(8,128)(2,1)S(1)} %copy-done, f32[1664]{0:T(1024)S(1)} %copy-done.6, f32[512]{0:T(512)S(1)} %add_rsqrt_fusion, f32[512]{0:T(512)S(1)} %broadcast_multiply_fusion), kind=kOutput, calls=%fused_computation.19 | convolution fusion | flops 4258562048 | bytes 12577280 | tf_op jit(solution)/shard_map/td,pdn->ptn/dot_general | solution.py:370
  100.9 1.3 fusion.17
  102.2 5.7 %fusion.29 = (f32[4,2,512]{2,1,0:T(2,128)S(1)}, f32[4,2,512,512]{2,3,1,0:T(8,128)}) fusion(f32[4,2,512,512]{2,3,1,0:T(8,128)S(1)} %fusion.17, pred[512,512]{0,1:T(8,128)(4,1)S(1)} %broadcast_compare_fusion), kind=kOutput, calls=%fused_computation.64 | output fusion | flops 12583423 | bytes 17055744 | tf_op jit(solution)/shard_map/sub | solution.py:353
  107.9 4.4 %fusion.16 = bf16[4,2,104,512]{3,2,1,0:T(8,128)(2,1)S(1)} fusion(f32[4,2,512,512]{2,3,1,0:T(8,128)} %get-tuple-element.14, f32[4,2,512]{2,1,0:T(2,128)S(1)} %get-tuple-element.13, bf16[4,512,3,2,104]{1,4,3,2,0:T(8,128)(2,1)S(1)} %bitcast.63), kind=kOutput, calls=%fused_computation.24 | convolution fusion | flops 440827904 | bytes 10108928 | tf_op jit(solution)/shard_map/phqk,pkhe->pqhe/dot_general | solution.py:355
  112.3 0.1 copy-done.5
  112.4 3.9 %fusion.30 = (f32[512]{0:T(512)S(1)}, f32[512,1664]{1,0:T(8,128)}) fusion(bf16[4,512,208]{1,2,0:T(8,128)(2,1)S(1)} %bitcast.73, bf16[4,1664,208]{2,1,0:T(8,128)(2,1)S(1)} %bitcast.72, bf16[512,1664]{1,0:T(8,128)(2,1)S(1)} %copy-done), kind=kOutput, calls=%fused_computation.65 | convolution fusion | flops 1420230144 | bytes 8734720 | tf_op jit(solution)/shard_map/ptn,pdn->td/dot_general | solution.py:372
  116.3 0.1 reduce_sum.72
  116.4 0.1 reduce_sum.73
  116.5 0.1 sub.42
  116.6 0.1 sub.43
  116.7 3.1 %reshape.136 = f32[128,6656]{1,0:T(8,128)S(1)} reshape(f32[512,1664]{1,0:T(8,128)} %get-tuple-element.16) | data formatting | bytes 6815744 | tf_op jit(solution)/shard_map/reshape | solution.py:374
  119.9 0.0 copy-start.2
  119.9 2.6 %multiply_reduce_fusion = f32[512]{0:T(512)S(1)} fusion(f32[512,1664]{1,0:T(8,128)} %get-tuple-element.16, f32[512]{0:T(512)S(1)} %sub.43), kind=kLoop, calls=%fused_computation.18 | loop fusion | flops 2555392 | bytes 3411968 | tf_op jit(solution)/shard_map/reduce_sum | solution.py:22
  122.5 0.1 reduce_sum.75
  122.6 0.1 reduce_sum.76
  122.8 1.8 select_convert_fusion.own
  124.6 0.6 collective-permute-start.1
  125.1 0.6 reduce-window.6
  125.7 0.2 slice_reduce_fusion
  126.0 0.1 fusion.24
  126.1 0.8 fusion.18.place
  126.9 37.3 %collective-permute-done.1.theirs = bf16[128,6656]{1,0:T(8,128)(2,1)S(1)} collective-permute-done((bf16[128,6656]{1,0:T(8,128)(2,1)}, bf16[128,6656]{1,0:T(8,128)(2,1)S(1)}, u32[]{:S(2)}, u32[]{:S(2)}) %collective-permute-start.1) | collective-permute-done | bytes 1703968 | tf_op jit(solution)/shard_map/ppermute | solution.py:377
  164.2 1.2 copy-done.1
  165.3 33.4 %shard_map.83 = bf16[512,1024]{1,0:T(8,128)(2,1)} custom-call(bf16[128,6656]{1,0:T(8,128)(2,1)} %select_convert_fusion.own, bf16[128,6656]{1,0:T(8,128)(2,1)} %copy-done.1, bf16[6656,1024]{1,0:T(8,128)(2,1)} %all-gather.2.cloned.1.call-done.weight, bf16[512,256]{1,0:T(8,128)(2,1)} %fusion.18.place), custom_call_target="tpu_custom_call" | custom-call | flops 3489660928 | bytes 13631488 | tf_op jit(solution)/shard_map/pallas_call | solution.py:304
  198.8 2.3 %copy.45 = bf16[512,1024]{1,0:T(8,128)(2,1)} copy(bf16[512,1024]{1,0:T(8,128)(2,1)} %shard_map.83) | data formatting | bytes 2097152
  (18 shorter events, 0.1 us)
Async XLA Ops:
  6.5 4.5 %copy-start.4 = (s32[1024]{0:T(1024)S(1)}, s32[1024]{0:T(1024)}, u32[]{:S(2)}) copy-start(s32[1024]{0:T(1024)} %param.14) | copy-start | bytes 12292
  6.5 4.8 %copy-start = (bf16[512,1664]{1,0:T(8,128)(2,1)S(1)}, bf16[512,1664]{1,0:T(8,128)(2,1)}, u32[]{:S(2)}) copy-start(bf16[512,1664]{1,0:T(8,128)(2,1)} %param.8) | copy-start | bytes 5111812
  6.5 157.6 %all-gather.2.cloned.1.call-start = ((), (), s32[]{:S(2)}) async-start(), calls=%async_computation | async-start | bytes 14483456 | tf_op jit(solution)/shard_map/all_gather | solution.py:364
  10.4 81.5 %copy-start.6 = (f32[1664]{0:T(1024)S(1)}, f32[1664]{0:T(1024)}, u32[]{:S(2)}) copy-start(f32[1664]{0:T(1024)} %param.9) | copy-start | bytes 19972
  10.5 2.0 collective-permute-start
  107.9 4.5 %copy-start.5 = (bf16[4,8,208,208]{3,2,1,0:T(8,128)(2,1)S(1)}, bf16[4,8,208,208]{3,2,1,0:T(8,128)(2,1)}, u32[]{:S(2)}) copy-start(bf16[4,8,208,208]{3,2,1,0:T(8,128)(2,1)} %get-tuple-element.8) | copy-start | bytes 8306692
  119.9 2.9 %copy-start.2 = (f32[6656]{0:T(1024)S(1)}, f32[6656]{0:T(1024)}, u32[]{:S(2)}) copy-start(f32[6656]{0:T(1024)} %param.12) | copy-start | bytes 79876
  122.5 2.6 %copy-start.3 = (s32[256,1]{0,1:T(1,128)S(1)}, s32[256,1]{0,1:T(1,128)}, u32[]{:S(2)}) copy-start(s32[256,1]{0,1:T(1,128)} %param.15) | copy-start | bytes 3076
  124.6 39.6 %collective-permute-start.1 = (bf16[128,6656]{1,0:T(8,128)(2,1)}, bf16[128,6656]{1,0:T(8,128)(2,1)S(1)}, u32[]{:S(2)}, u32[]{:S(2)}) collective-permute-start(bf16[128,6656]{1,0:T(8,128)(2,1)} %select_convert_fusion.own), channel_id=1, source_target_pairs={{0,1},{1,0},{2,3},{3,2},{4,5},{5,4},{6,7},{7,6},{8,9},{9,8},{10,11... | collective-permute-start | bytes 5111816 | tf_op jit(solution)/shard_map/ppermute | solution.py:377
  164.2 1.2 copy-start.1
Sparse Core Ops, SparseCore 0:
  9.7 133.3 all-gather.1

commit v3 on v2

--- a/solution.py
+++ b/solution.py
@@ -220,17 +220,21 @@
 TAIL_COLS = 256
 
 
-def tail_kernel(own, theirs, weight, place, out, rows, wide, feat, load_sem, keep_sem, send_sem, recv_sem):
+def tail_kernel(parts, *refs):
+    merge_parts(refs[:parts], *refs[parts:])
+
+
+def merge_parts(pieces, weight, place, out, rows, wide, feat, load_sem, keep_sem, send_sem, recv_sem):
     x = lax.axis_index("inner")
     me = lax.axis_index("dp")
     peers = lax.axis_size("dp")
-    half = own.shape[0]
+    piece = pieces[0].shape[0]
     slots = out.shape[0] // peers
     chunks = weight.shape[1] // TAIL_COLS
 
     loads = [
-        pltpu.make_async_copy(own, rows.at[pl.ds(0, half)], load_sem.at[chunks]),
-        pltpu.make_async_copy(theirs, rows.at[pl.ds(half, half)], load_sem.at[chunks + 1]),
+        pltpu.make_async_copy(ref, rows.at[pl.ds(number * piece, piece)], load_sem.at[chunks + number])
+        for number, ref in enumerate(pieces)
     ]
     for chunk in range(chunks):
         loads.append(
@@ -245,12 +249,12 @@
     for step in range(1, peers):
         other = lax.rem(me + step, peers)
         pl.semaphore_signal(barrier, inc=1, device_id=(other, x), device_id_type=MESH)
-    loads[0].wait()
-    loads[1].wait()
+    for number in range(len(pieces)):
+        loads[number].wait()
 
     copies = []
     for chunk in range(chunks):
-        loads[2 + chunk].wait()
+        loads[len(pieces) + chunk].wait()
         product = jnp.dot(rows[...], wide[chunk], preferred_element_type=jnp.float32)
         feat[chunk] = jnp.dot(
             place[...], product.astype(jnp.bfloat16), preferred_element_type=jnp.float32
@@ -296,32 +300,33 @@
             copy.wait_send()
 
 
-def merge_and_route(own, theirs, weight, place):
+def merge_and_route(pieces, weight, place, collective_id):
     peers = lax.axis_size("dp")
     out_rows, group = place.shape
     depth, columns = weight.shape
     chunks = columns // TAIL_COLS
     return pl.pallas_call(
-        tail_kernel,
+        functools.partial(tail_kernel, len(pieces)),
         out_shape=jax.ShapeDtypeStruct((out_rows, columns), jnp.bfloat16),
-        in_specs=[pl.BlockSpec(memory_space=pl.ANY)] * 3 + [pl.BlockSpec(memory_space=pltpu.VMEM)],
-        out_specs=pl.BlockSpec(memory_space=pl.ANY),
+        in_specs=[pl.BlockSpec(memory_space=pltpu.VMEM)] * len(pieces)
+        + [pl.BlockSpec(memory_space=pl.ANY), pl.BlockSpec(memory_space=pltpu.VMEM)],
+        out_specs=pl.BlockSpec(memory_space=pltpu.VMEM),
         scratch_shapes=[
             pltpu.VMEM((group, depth), jnp.bfloat16),
             pltpu.VMEM((chunks, depth, TAIL_COLS), jnp.bfloat16),
             pltpu.VMEM((chunks, out_rows, TAIL_COLS), jnp.bfloat16),
-            pltpu.SemaphoreType.DMA((chunks + 2,)),
+            pltpu.SemaphoreType.DMA((chunks + len(pieces),)),
             pltpu.SemaphoreType.DMA((chunks,)),
             pltpu.SemaphoreType.DMA((chunks, peers)),
             pltpu.SemaphoreType.DMA((chunks, peers)),
         ],
         compiler_params=pltpu.CompilerParams(
-            collective_id=1, has_side_effects=True, vmem_limit_bytes=56 * 1024 * 1024
+            collective_id=collective_id, has_side_effects=True, vmem_limit_bytes=56 * 1024 * 1024
         ),
         cost_estimate=pl.CostEstimate(
             flops=2 * group * depth * columns, bytes_accessed=2 * depth * columns, transcendentals=0
         ),
-    )(own, theirs, weight, place)
+    )(*pieces, weight, place)
 
 
 def pair_shards(qkv_weight, out_weight):
@@ -341,13 +346,11 @@
     return shard[:, : 3 * half], shard[:, 3 * half :]
 
 
-def attend_pairs(projected, segment):
-    pairs, rows, width = projected.shape
-    shaped = projected.reshape(pairs, rows, 3, 2, HEAD_DIM)
-    queries, keys, vectors = shaped[:, :, 0], shaped[:, :, 1], shaped[:, :, 2]
+def attend_pairs(queries, keys, vectors, own_segment, segment):
+    pairs, rows = queries.shape[:2]
     scale = HEAD_DIM ** (-0.5)
     scores = jnp.einsum("pqhe,pkhe->phqk", queries, keys, preferred_element_type=jnp.float32) * scale
-    visible = segment[:, None] == segment[None, :]
+    visible = own_segment[:, None] == segment[None, :]
     scores = jnp.where(visible[None, None], scores, NEG)
     top = jnp.max(scores, axis=-1, keepdims=True)
     weights = jnp.exp(scores - top)
@@ -361,22 +364,36 @@
     local_segment = lax.dynamic_slice_in_dim(
         segment_ids, lax.axis_index("inner") * tok_rows, tok_rows
     )
-    merge_full = lax.all_gather(merge_weight, "dp", axis=0, tiled=True)
+    cut = merge_weight.shape[1] // 2
+    merge_halves = [
+        lax.all_gather(merge_weight[:, part * cut : (part + 1) * cut], "dp", axis=0, tiled=True)
+        for part in range(2)
+    ]
     sq, so = pair_shards(qkv_weight, out_weight)
     gq, go = gather_heads(sq, so)
     gq = gq.reshape(4, width, sq.shape[1])
     go = go.reshape(4, width, so.shape[1])
     normed = layer_norm(tokens, attn_gain).astype(jnp.bfloat16)
     projected = jnp.einsum("td,pdn->ptn", normed, gq, preferred_element_type=jnp.float32)
-    context = attend_pairs(projected.astype(jnp.bfloat16), local_segment)
-    attn_out = jnp.einsum("ptn,pdn->td", context, go, preferred_element_type=jnp.float32)
-    hidden = tokens.astype(jnp.float32) + attn_out
-    quad_rows = hidden.reshape(tok_rows // 4, -1)
+    shaped = projected.astype(jnp.bfloat16).reshape(4, tok_rows, 3, 2, HEAD_DIM)
+    queries, keys, vectors = shaped[:, :, 0], shaped[:, :, 1], shaped[:, :, 2]
     live = local_segment.reshape(-1, 4)[:, 0] >= 0
-    merged = jnp.where(live[:, None], layer_norm(quad_rows, merge_gain), 0.0).astype(jnp.bfloat16)
-    theirs = lax.ppermute(merged, "inner", [(0, 1), (1, 0)])
+    step = tok_rows // 2
+    own, theirs = [], []
+    for start in range(0, tok_rows, step):
+        rows = slice(start, start + step)
+        asking = queries[:, rows]
+        if own:
+            asking, own[-1] = lax.optimization_barrier((asking, own[-1]))
+        context = attend_pairs(asking, keys, vectors, local_segment[rows], local_segment)
+        attn_out = jnp.einsum("ptn,pdn->td", context, go, preferred_element_type=jnp.float32)
+        hidden = tokens[rows].astype(jnp.float32) + attn_out
+        normal = layer_norm(hidden.reshape(step // 4, -1), merge_gain)
+        merged = jnp.where(live[start // 4 : (start + step) // 4, None], normal, 0.0)
+        own.append(merged.astype(jnp.bfloat16))
+        theirs.append(lax.ppermute(own[-1], "inner", [(0, 1), (1, 0)]))
     n_dp = lax.axis_size("dp")
-    half_rows = merged.shape[0]
+    half_rows = tok_rows // 4
     slots = 4 * half_rows // n_dp
     owner_col = owners[:, 0]
     chosen = (owner_col[:, None] == jnp.arange(n_dp, dtype=jnp.int32)[None, :]).astype(jnp.int32)
@@ -389,7 +406,10 @@
         jnp.concatenate([target[half_rows:], target[:half_rows]]),
     )
     place = (jnp.arange(n_dp * slots, dtype=jnp.int32)[:, None] == target[None, :]).astype(jnp.bfloat16)
-    return merge_and_route(merged, theirs, merge_full, place)
+    first = merge_and_route(own + theirs, merge_halves[0], place, 1)
+    place, _ = lax.optimization_barrier((place, first))
+    second = merge_and_route(own + theirs, merge_halves[1], place, 2)
+    return jnp.concatenate([first, second], axis=1)
 
 
 def solution(mesh):

time: 208 us -> 210 us (level)
  waiting for transfers between devices: 38 us -> 22.2 us
  Pallas kernels: 111 us -> 120 us
  local copies, waits for them, and re-layouts: 10.5 us -> 16.8 us
    ppermute x1 -> x2, waiting for transfers between devices: 37.3 us -> 22.1 us  [local_ring(): theirs.append(lax.ppermute(own[-1], 'inner', [(0, 1), (1, 0)]))]
    pallas_call x1 -> x2, Pallas kernels: 33.4 us -> 43.6 us  [merge_and_route(): pl.pallas_call(functools.partial(tail_kernel, len(pieces)), out_shape=jax...]
    slice x1 -> x5, local copies, waits for them, and re-layouts: 0.18 us -> 4.01 us  [the longest x1 2.32 us: local_ring(): merge_weight[:, part * cut:(part + 1) * cut]]
    concatenate x0 -> x1, other arithmetic: none -> 2.12 us  [local_ring(): return jnp.concatenate([first, second], axis=1)]
    reshape x1 -> x2, local copies, waits for them, and re-layouts: 3.1 us -> 4.8 us  [local_ring(): normal = layer_norm(hidden.reshape(step // 4, -1), merge_gain)]
    sub x1 -> x2, other arithmetic: 5.67 us -> 4.34 us  [attend_pairs(): weights = jnp.exp(scores - top)]
    dot_general x1 -> x2, matrix products: 4.38 us -> 3.19 us  [attend_pairs(): jnp.einsum('phqk,pkhe->pqhe', probs, vectors, preferred_element_type=jnp....]
  transfers between devices with their start and end apart: 3 -> 5, of which waited for: 1 -> 1; matrix products, arithmetic and copies ran while one was open for 19% -> 21% of each run, Pallas kernels for 37% -> 47%
where the time goes in v3:
time: 210 us
  Pallas kernels  120 us (57%)
  waiting for transfers between devices  22.2 us (11%)
  matrix products  18.8 us (9%)
  local copies, waits for them, and re-layouts  16.8 us (8%)
  other arithmetic  16.3 us (8%)
  between operations  13.8 us (7%)
  starting transfers between devices  2.26 us (1%)
    pallas_call x1, Pallas kernels, gather_heads(): pl.pallas_call(gather_kernel, out_shape=(jax.ShapeDtypeStruct((4, RING) +...  76.1 us
    pallas_call x2, Pallas kernels, merge_and_route(): pl.pallas_call(functools.partial(tail_kernel, len(pieces)), out_shape=jax...  43.6 us
    ppermute x2, waiting for transfers between devices, local_ring(): theirs.append(lax.ppermute(own[-1], 'inner', [(0, 1), (1, 0)]))  22.1 us
    dot_general x1, matrix products, local_ring(): jnp.einsum('td,pdn->ptn', normed, gq, preferred_element_type=jnp.float32)  9.07 us
    reshape x2, local copies, waits for them, and re-layouts, local_ring(): normal = layer_norm(hidden.reshape(step // 4, -1), merge_gain)  4.8 us
    sub x2, other arithmetic, attend_pairs(): weights = jnp.exp(scores - top)  4.34 us
  transfers between devices with their start and end apart: 5, of which 1 were waited for; matrix products, arithmetic and copies ran while one was open for 21% of the time, Pallas kernels for 47%

profile of v3, /device:TPU:0, one launch (start us, length us, event | category | flops | bytes accessed | tf_op | source)
XLA Modules:
  0.0 209.8 jit_solution(9330723884510181322)
XLA Ops:
  6.6 2.3 %fusion.40 = (bf16[416,512]{1,0:T(8,128)(2,1)}, bf16[416,512]{1,0:T(8,128)(2,1)}) fusion(bf16[416,1024]{1,0:T(8,128)(2,1)} %param.13), kind=kLoop, calls=%fused_computation.87 | loop fusion | bytes 1703936 | tf_op jit(solution)/shard_map/slice | solution.py:369
  9.0 1.2 reshape.182
  10.2 0.7 copy.26
  10.9 0.2 copy.28
  11.2 0.1 select_bitcast_fusion
  11.3 0.5 collective-permute-start
  12.1 0.6 reduce-window.6
  12.7 0.2 slice_reduce_fusion.2
  12.9 0.6 slice_reduce_fusion
  13.7 0.3 convert_reduce_fusion
  14.0 0.2 broadcast_compare_fusion
  14.2 0.6 fusion.4
  14.8 0.2 bitcast_select_fusion
  15.0 0.7 pad_maximum_fusion.2.so
  15.7 0.7 fusion.30.sq
  16.5 76.1 %shard_map.82 = (bf16[4,8,208,624]{3,2,1,0:T(8,128)(2,1)}, bf16[4,8,208,208]{3,2,1,0:T(8,128)(2,1)}) custom-call(bf16[208,624]{1,0:T(8,128)(2,1)} %fusion.30.sq, bf16[208,208]{1,0:T(8,128)(2,1)} %pad_maximum_fusion.2.so), custom_call_target="tpu_custom_call" | custom-call | bytes 200000000 | tf_op jit(solution)/shard_map/pallas_call | solution.py:202
  92.5 9.1 %convolution_convert_fusion = bf16[4,624,512]{2,1,0:T(8,128)(2,1)S(1)} fusion(bf16[4,1664,624]{2,1,0:T(8,128)(2,1)} %bitcast.87, bf16[512,1664]{1,0:T(8,128)(2,1)S(1)} %copy-done.2, f32[1664]{0:T(1024)S(1)} %copy-done.16, f32[512]{0:T(512)S(1)} %add_rsqrt_fusion, f32[512]{0:T(512)S(1)} %broadcast_multiply_fusion), kind=kOutput, calls=%fused_computation.29 | convolution fusion | flops 4258562048 | bytes 12577280 | tf_op jit(solution)/shard_map/td,pdn->ptn/dot_general | solution.py:377
  101.7 0.9 slice.103
  102.6 0.8 fusion.27
  103.3 2.2 %fusion.43 = (f32[4,2,256]{2,1,0:T(2,128)S(1)}, f32[4,2,256,512]{3,2,1,0:T(8,128)S(1)}) fusion(f32[4,2,256,512]{3,2,1,0:T(8,128)S(1)} %fusion.27, pred[256,512]{1,0:T(8,128)(4,1)S(1)} %get-tuple-element.22), kind=kOutput, calls=%fused_computation.90 | output fusion | flops 6291967 | bytes 8527872 | tf_op jit(solution)/shard_map/sub | solution.py:356
  105.5 0.9 fusion.25
  106.4 1.0 copy-done.14
  107.5 1.3 fusion.44
  108.8 0.7 reduce_sum.113
  109.5 0.9 reduce_sum.114
  110.4 0.5 copy-done.11
  110.9 0.7 sub.67
  111.6 0.9 sub.68
  112.5 1.4 reshape.190
  113.9 0.3 multiply_reduce_fusion.1
  114.5 1.8 select_convert_fusion.1.refs_0_
  116.3 0.7 collective-permute-start.1
  117.1 2.0 fusion.26
  119.1 2.2 %fusion.45 = (f32[4,2,256]{2,1,0:T(2,128)S(1)}, f32[4,2,256,512]{3,2,1,0:T(8,128)S(1)}) fusion(f32[4,2,256,512]{3,2,1,0:T(8,128)S(1)} %fusion.26, pred[256,512]{1,0:T(8,128)(4,1)S(1)} %get-tuple-element.21), kind=kOutput, calls=%fused_computation.92 | output fusion | flops 6291967 | bytes 8527872 | tf_op jit(solution)/shard_map/sub | solution.py:356
  121.3 2.3 %fusion.24 = bf16[4,2,104,256]{3,2,1,0:T(8,128)(2,1)S(1)} fusion(f32[4,2,256,512]{3,2,1,0:T(8,128)S(1)} %get-tuple-element.32, f32[4,2,256]{2,1,0:T(2,128)S(1)} %get-tuple-element.31, bf16[4,512,3,2,104]{1,4,3,2,0:T(8,128)(2,1)} %bitcast.79), kind=kOutput, calls=%fused_computation.38 | convolution fusion | flops 220413952 | bytes 5480448 | tf_op jit(solution)/shard_map/phqk,pkhe->pqhe/dot_general | solution.py:358
  123.6 2.4 %fusion.46 = (f32[256]{0:T(256)S(1)}, f32[256,1664]{1,0:T(8,128)}) fusion(bf16[4,256,208]{1,2,0:T(8,128)(2,1)S(1)} %bitcast.90, bf16[4,1664,208]{2,1,0:T(8,128)(2,1)S(1)} %bitcast.89, bf16[512,1664]{1,0:T(8,128)(2,1)S(1)} %copy-done.2), kind=kOutput, calls=%fused_computation.93 | convolution fusion | flops 710115072 | bytes 5751808 | tf_op jit(solution)/shard_map/ptn,pdn->td/dot_general | solution.py:389
  126.3 0.1 sub.76
  126.4 3.4 %reshape.192 = f32[64,6656]{1,0:T(8,128)} reshape(f32[256,1664]{1,0:T(8,128)} %get-tuple-element.34) | data formatting | bytes 3407872 | tf_op jit(solution)/shard_map/reshape | solution.py:391
  129.8 0.3 multiply_reduce_fusion
  130.4 1.8 select_convert_fusion.refs_1_
  132.1 0.9 collective-permute-start.2
  133.1 0.8 fusion.28.refs_5_
  133.9 22.1 %collective-permute-done.2.refs_3_ = bf16[64,6656]{1,0:T(8,128)(2,1)S(1)} collective-permute-done((bf16[64,6656]{1,0:T(8,128)(2,1)S(1)}, bf16[64,6656]{1,0:T(8,128)(2,1)S(1)}, u32[]{:S(2)}, u32[]{:S(2)}) %collective-permute-start.2) | collective-permute-done | bytes 852000 | tf_op jit(solution)/shard_map/ppermute | solution.py:394
  156.0 0.8 copy-done.5
  156.9 0.3 copy-done.4
  157.2 22.4 %shard_map.83 = bf16[512,512]{1,0:T(8,128)(2,1)} custom-call(bf16[64,6656]{1,0:T(8,128)(2,1)} %copy-done, bf16[64,6656]{1,0:T(8,128)(2,1)} %copy-done.1, bf16[64,6656]{1,0:T(8,128)(2,1)} %copy-done.4, bf16[64,6656]{1,0:T(8,128)(2,1)} %copy-done.5, bf16[6656,512]{1,0:T(8,128)(2,1)} %all-gather.3.cloned.1.call-done.refs_4_, bf16[512,256]{1,0:T(8,128)(2,1)} %fusion.28.refs_5_), custom_call_target="tpu_custom_call" | custom-call | flops 1744830464 | bytes 6815744 | tf_op jit(solution)/shard_map/pallas_call | solution.py:308
  179.6 21.1 %shard_map.84 = bf16[512,512]{1,0:T(8,128)(2,1)} custom-call(bf16[64,6656]{1,0:T(8,128)(2,1)} %copy-done, bf16[64,6656]{1,0:T(8,128)(2,1)} %copy-done.1, bf16[64,6656]{1,0:T(8,128)(2,1)} %copy-done.4, bf16[64,6656]{1,0:T(8,128)(2,1)} %copy-done.5, bf16[6656,512]{1,0:T(8,128)(2,1)} %all-gather.5.cloned.1.call-done.refs_4_, bf16[512,256]{1,0:T(8,128)(2,1)} %fusion.28.refs_5_), custom_call_target="tpu_custom_call" | custom-call | flops 1744830464 | bytes 6815744 | tf_op jit(solution)/shard_map/pallas_call | solution.py:308
  200.8 2.1 %pad_maximum_fusion = bf16[512,1024]{1,0:T(8,128)(2,1)} fusion(bf16[512,512]{1,0:T(8,128)(2,1)} %shard_map.84, bf16[512,512]{1,0:T(8,128)(2,1)S(1)} %copy-done.7), kind=kLoop, calls=%fused_computation.40 | loop fusion | flops 2097152 | bytes 2097152 | tf_op jit(solution)/shard_map/concatenate | solution.py:412
  (64 shorter events, 1.5 us)
Async XLA Ops:
  6.5 4.6 %copy-start.9 = (bf16[416,104]{1,0:T(8,128)(2,1)S(1)}, bf16[416,104]{1,0:T(8,128)(2,1)}, u32[]{:S(2)}) copy-start(bf16[416,104]{1,0:T(8,128)(2,1)} %param.11) | copy-start | bytes 259588
  6.5 5.4 %copy-start.13 = (s32[1024]{0:T(1024)S(1)}, s32[1024]{0:T(1024)}, u32[]{:S(2)}) copy-start(s32[1024]{0:T(1024)} %param.14) | copy-start | bytes 12292
  6.5 5.6 %copy-start.10 = (s32[256,1]{0,1:T(1,128)S(1)}, s32[256,1]{0,1:T(1,128)}, u32[]{:S(2)}) copy-start(s32[256,1]{0,1:T(1,128)} %param.15) | copy-start | bytes 3076
  6.5 7.1 %copy-start.2 = (bf16[512,1664]{1,0:T(8,128)(2,1)S(1)}, bf16[512,1664]{1,0:T(8,128)(2,1)}, u32[]{:S(2)}) copy-start(bf16[512,1664]{1,0:T(8,128)(2,1)} %param.8) | copy-start | bytes 5111812
  6.5 149.4 %all-gather.3.cloned.1.call-start = ((), (), s32[]{:S(2)}) async-start(), calls=%async_computation | async-start | bytes 7241728 | tf_op jit(solution)/shard_map/all_gather | solution.py:369
  8.9 170.7 %all-gather.5.cloned.1.call-start = ((), (), s32[]{:S(2)}) async-start(), calls=%async_computation.1 | async-start | bytes 7241728 | tf_op jit(solution)/shard_map/all_gather | solution.py:369
  11.3 3.5 %collective-permute-start = (bf16[104,832]{1,0:T(8,128)(2,1)S(1)}, bf16[104,832]{1,0:T(8,128)(2,1)S(1)}, u32[]{:S(2)}, u32[]{:S(2)}) collective-permute-start(bf16[104,832]{1,0:T(8,128)(2,1)S(1)} %select_bitcast_fusion), channel_id=1, source_target_pairs={{0,2},{2,0},{4,6},{6,4},{8,10},{10,8},{12,14},{14,12},{16,18},{18,... | collective-permute-start | bytes 519176 | tf_op jit(solution)/shard_map/ppermute | solution.py:342
  11.9 80.7 %copy-start.16 = (f32[1664]{0:T(1024)S(1)}, f32[1664]{0:T(1024)}, u32[]{:S(2)}) copy-start(f32[1664]{0:T(1024)} %param.9) | copy-start | bytes 19972
  101.6 3.9 %copy-start.6 = (bf16[4,624,512]{2,1,0:T(8,128)(2,1)}, bf16[4,624,512]{2,1,0:T(8,128)(2,1)S(1)}, u32[]{:S(2)}) copy-start(bf16[4,624,512]{2,1,0:T(8,128)(2,1)S(1)} %convolution_convert_fusion) | copy-start | bytes 7667716
  105.5 2.0 copy-start.14
  110.4 0.5 copy-start.11
  116.3 5.0 %copy-start = (bf16[64,6656]{1,0:T(8,128)(2,1)}, bf16[64,6656]{1,0:T(8,128)(2,1)S(1)}, u32[]{:S(2)}) copy-start(bf16[64,6656]{1,0:T(8,128)(2,1)S(1)} %select_convert_fusion.1.refs_0_) | copy-start | bytes 2555908
  116.3 39.7 %collective-permute-start.1 = (bf16[64,6656]{1,0:T(8,128)(2,1)S(1)}, bf16[64,6656]{1,0:T(8,128)(2,1)S(1)}, u32[]{:S(2)}, u32[]{:S(2)}) collective-permute-start(bf16[64,6656]{1,0:T(8,128)(2,1)S(1)} %select_convert_fusion.1.refs_0_), channel_id=1, source_target_pairs={{0,1},{1,0},{2,3},{3,2},{4,5},{5,4},{6,7},{7,6},{8,9},{9,8},{10,11... | collective-permute-start | bytes 2555912 | tf_op jit(solution)/shard_map/ppermute | solution.py:394
  121.3 2.3 %copy-start.15 = (bf16[4,8,208,208]{3,2,1,0:T(8,128)(2,1)S(1)}, bf16[4,8,208,208]{3,2,1,0:T(8,128)(2,1)}, u32[]{:S(2)}) copy-start(bf16[4,8,208,208]{3,2,1,0:T(8,128)(2,1)} %get-tuple-element.11) | copy-start | bytes 8306692
  126.0 3.8 %copy-start.3 = (f32[256,1664]{1,0:T(8,128)S(1)}, f32[256,1664]{1,0:T(8,128)}, u32[]{:S(2)}) copy-start(f32[256,1664]{1,0:T(8,128)} %get-tuple-element.34) | copy-start | bytes 5111812
  126.0 4.3 %copy-start.8 = (f32[6656]{0:T(1024)S(1)}, f32[6656]{0:T(1024)}, u32[]{:S(2)}) copy-start(f32[6656]{0:T(1024)} %param.12) | copy-start | bytes 79876
  126.0 4.3 %copy-start.12 = (pred[64]{0:T(512)(128)(4,1)S(1)}, pred[64]{0:T(512)(128)(4,1)}, u32[]{:S(2)}) copy-start(pred[64]{0:T(512)(128)(4,1)} %get-tuple-element.15) | copy-start | bytes 196
  132.1 23.9 %copy-start.1 = (bf16[64,6656]{1,0:T(8,128)(2,1)}, bf16[64,6656]{1,0:T(8,128)(2,1)S(1)}, u32[]{:S(2)}) copy-start(bf16[64,6656]{1,0:T(8,128)(2,1)S(1)} %select_convert_fusion.refs_1_) | copy-start | bytes 2555908
  132.1 23.8 %collective-permute-start.2 = (bf16[64,6656]{1,0:T(8,128)(2,1)S(1)}, bf16[64,6656]{1,0:T(8,128)(2,1)S(1)}, u32[]{:S(2)}, u32[]{:S(2)}) collective-permute-start(bf16[64,6656]{1,0:T(8,128)(2,1)S(1)} %select_convert_fusion.refs_1_), channel_id=1, source_target_pairs={{0,1},{1,0},{2,3},{3,2},{4,5},{5,4},{6,7},{7,6},{8,9},{9,8},{10,11... | collective-permute-start | bytes 2555912 | tf_op jit(solution)/shard_map/ppermute | solution.py:394
  156.0 0.9 copy-start.5
  156.0 1.2 copy-start.4
  179.6 21.2 %copy-start.7 = (bf16[512,512]{1,0:T(8,128)(2,1)S(1)}, bf16[512,512]{1,0:T(8,128)(2,1)}, u32[]{:S(2)}) copy-start(bf16[512,512]{1,0:T(8,128)(2,1)} %shard_map.83) | copy-start | bytes 1572868
Sparse Core Ops, SparseCore 0:
  9.7 82.9 all-gather.2
  94.9 66.5 all-gather.4

commit v4 on v3

--- a/solution.py
+++ b/solution.py
@@ -159,33 +159,37 @@
             device_id_type=MESH,
         ).wait_recv()
 
-    def spread(a, dist):
+    def spread(a, plane, dist):
         index = dist % RING
-        send(a, 8 + index, mine, dist, across)
-        send(a, 16 + index, mine, dist, sibling)
+        if a == 0:
+            send(a, 8 + index, plane, dist, across)
+        send(a, (16 if plane is mine else 24) + index, plane, dist, sibling)
 
     top, bottom = (0, split), (split, sq.shape[0] - split)
-    for a in range(2):
-        send(a, 0, mine, 0, right)
-        send(a, 4, mine, 0, left)
-        spread(a, 0)
+    rings = ((0, mine, 0), (1, mine, 0), (1, far, 32))
+    send(1, 8, mine, 0, across)
+    for a, plane, base in rings:
+        if plane is far:
+            arrived(1, 8, far, 0, across)
+        send(a, base, plane, 0, right)
+        send(a, base + 4, plane, 0, left)
+        spread(a, plane, 0)
     for step in range(1, 4):
-        for a in range(2):
-            arrived(a, step - 1, mine, -step, left)
-            send(a, step, mine, -step, right, top if step == 3 else None)
-            spread(a, -step)
-            arrived(a, 4 + step - 1, mine, step, right)
-            send(a, 4 + step, mine, step, left, bottom if step == 3 else None)
-            spread(a, step)
-    for a in range(2):
-        arrived(a, 3, mine, 4, left, top)
-        arrived(a, 7, mine, 4, right, bottom)
-        spread(a, 4)
+        for a, plane, base in rings:
+            arrived(a, base + step - 1, plane, -step, left)
+            send(a, base + step, plane, -step, right, top if step == 3 else None)
+            spread(a, plane, -step)
+            arrived(a, base + 4 + step - 1, plane, step, right)
+            send(a, base + 4 + step, plane, step, left, bottom if step == 3 else None)
+            spread(a, plane, step)
+    for a, plane, base in rings:
+        arrived(a, base + 3, plane, 4, left, top)
+        arrived(a, base + 7, plane, 4, right, bottom)
+        spread(a, plane, 4)
     order = (0, -1, 1, -2, 2, -3, 3, 4)
     for dist in order:
-        for a in range(2):
-            arrived(a, 8 + dist % RING, far, dist, across)
-            send(a, 24 + dist % RING, far, dist, sibling)
+        arrived(0, 8 + dist % RING, far, dist, across)
+        send(0, 24 + dist % RING, far, dist, sibling)
     near_other = 2 * x + 1 - core
     far_other = 2 * (1 - x) + 1 - core
     for dist in order:
@@ -209,8 +213,8 @@
         out_specs=(pl.BlockSpec(memory_space=pl.ANY),) * 2,
         scratch_shapes=[
             pltpu.SemaphoreType.DMA((2,)),
-            pltpu.SemaphoreType.DMA((2, 32)),
-            pltpu.SemaphoreType.DMA((2, 32)),
+            pltpu.SemaphoreType.DMA((2, 40)),
+            pltpu.SemaphoreType.DMA((2, 40)),
         ],
         compiler_params=pltpu.CompilerParams(collective_id=0, has_side_effects=True),
         cost_estimate=pl.CostEstimate(flops=0, bytes_accessed=200_000_000, transcendentals=0),
@@ -300,7 +304,7 @@
             copy.wait_send()
 
 
-def merge_and_route(pieces, weight, place, collective_id):
+def merge_and_route(pieces, weight, place):
     peers = lax.axis_size("dp")
     out_rows, group = place.shape
     depth, columns = weight.shape
@@ -321,7 +325,7 @@
             pltpu.SemaphoreType.DMA((chunks, peers)),
         ],
         compiler_params=pltpu.CompilerParams(
-            collective_id=collective_id, has_side_effects=True, vmem_limit_bytes=56 * 1024 * 1024
+            collective_id=1, has_side_effects=True, vmem_limit_bytes=56 * 1024 * 1024
         ),
         cost_estimate=pl.CostEstimate(
             flops=2 * group * depth * columns, bytes_accessed=2 * depth * columns, transcendentals=0
@@ -364,11 +368,7 @@
     local_segment = lax.dynamic_slice_in_dim(
         segment_ids, lax.axis_index("inner") * tok_rows, tok_rows
     )
-    cut = merge_weight.shape[1] // 2
-    merge_halves = [
-        lax.all_gather(merge_weight[:, part * cut : (part + 1) * cut], "dp", axis=0, tiled=True)
-        for part in range(2)
-    ]
+    merge_full = lax.all_gather(merge_weight, "dp", axis=0, tiled=True)
     sq, so = pair_shards(qkv_weight, out_weight)
     gq, go = gather_heads(sq, so)
     gq = gq.reshape(4, width, sq.shape[1])
@@ -406,10 +406,7 @@
         jnp.concatenate([target[half_rows:], target[:half_rows]]),
     )
     place = (jnp.arange(n_dp * slots, dtype=jnp.int32)[:, None] == target[None, :]).astype(jnp.bfloat16)
-    first = merge_and_route(own + theirs, merge_halves[0], place, 1)
-    place, _ = lax.optimization_barrier((place, first))
-    second = merge_and_route(own + theirs, merge_halves[1], place, 2)
-    return jnp.concatenate([first, second], axis=1)
+    return merge_and_route(own + theirs, merge_full, place)
 
 
 def solution(mesh):

time: 210 us -> 203 us (0.967)
  Pallas kernels: 120 us -> 113 us
  waiting for transfers between devices: 22.2 us -> 27.8 us
  other arithmetic: 16.3 us -> 13.6 us
  local copies, waits for them, and re-layouts: 16.8 us -> 14.5 us
    pallas_call x2 -> x1, Pallas kernels: 43.6 us -> 35.1 us  [merge_and_route(): pl.pallas_call(functools.partial(tail_kernel, len(pieces)), out_shape=jax...]
    ppermute x2, waiting for transfers between devices: 22.1 us -> 27.1 us  [local_ring(): theirs.append(lax.ppermute(own[-1], 'inner', [(0, 1), (1, 0)]))]
    reshape x2, local copies, waits for them, and re-layouts: 4.8 us -> 1.69 us  [local_ring(): normal = layer_norm(hidden.reshape(step // 4, -1), merge_gain)]
    slice x2 -> x1, local copies, waits for them, and re-layouts: 2.5 us -> 0.18 us  [the longest x1 2.32 us: local_ring(): merge_weight[:, part * cut:(part + 1) * cut]]
    unnamed x34 -> x25, local copies, waits for them, and re-layouts: 2.75 us -> 4.94 us
    concatenate x1 -> x0, other arithmetic: 2.12 us -> none  [local_ring(): return jnp.concatenate([first, second], axis=1)]
  transfers between devices with their start and end apart: 5 -> 4, of which waited for: 1 -> 1; matrix products, arithmetic and copies ran while one was open for 21% -> 20% of each run, Pallas kernels for 47% -> 38%
where the time goes in v4:
time: 203 us
  Pallas kernels  113 us (56%)
  waiting for transfers between devices  27.8 us (14%)
  matrix products  18 us (9%)
  local copies, waits for them, and re-layouts  14.5 us (7%)
  between operations  13.8 us (7%)
  other arithmetic  13.6 us (7%)
  starting transfers between devices  2.48 us (1%)
    pallas_call x1, Pallas kernels, gather_heads(): pl.pallas_call(gather_kernel, out_shape=(jax.ShapeDtypeStruct((4, RING) +...  77.5 us
    pallas_call x1, Pallas kernels, merge_and_route(): pl.pallas_call(functools.partial(tail_kernel, len(pieces)), out_shape=jax...  35.1 us
    ppermute x2, waiting for transfers between devices, local_ring(): theirs.append(lax.ppermute(own[-1], 'inner', [(0, 1), (1, 0)]))  27.1 us
    dot_general x1, matrix products, local_ring(): jnp.einsum('td,pdn->ptn', normed, gq, preferred_element_type=jnp.float32)  9.09 us
    unnamed x25, local copies, waits for them, and re-layouts  4.94 us
    sub x2, other arithmetic, attend_pairs(): weights = jnp.exp(scores - top)  4.34 us
  transfers between devices with their start and end apart: 4, of which 1 were waited for; matrix products, arithmetic and copies ran while one was open for 20% of the time, Pallas kernels for 38%

profile of v4, /device:TPU:0, one launch (start us, length us, event | category | flops | bytes accessed | tf_op | source)
XLA Modules:
  0.0 202.8 jit_solution(4643020508738388927)
XLA Ops:
  6.5 0.7 all-gather.2.cloned.1.call-update
  7.3 1.2 reshape.182
  8.5 0.7 copy.26
  9.2 0.2 copy.28
  9.4 1.0 copy.27
  10.4 0.1 select_bitcast_fusion
  10.5 0.5 collective-permute-start
  11.2 0.6 reduce-window.6
  11.8 0.2 slice_reduce_fusion.2
  12.1 0.7 slice_reduce_fusion
  12.9 0.3 convert_reduce_fusion
  13.2 0.2 broadcast_compare_fusion
  13.4 0.6 fusion.4
  14.0 0.2 bitcast_select_fusion
  14.2 0.7 pad_maximum_fusion.1.so
  14.9 0.7 fusion.30.sq
  15.7 77.5 %shard_map.82 = (bf16[4,8,208,624]{3,2,1,0:T(8,128)(2,1)}, bf16[4,8,208,208]{3,2,1,0:T(8,128)(2,1)}) custom-call(bf16[208,624]{1,0:T(8,128)(2,1)} %fusion.30.sq, bf16[208,208]{1,0:T(8,128)(2,1)} %pad_maximum_fusion.1.so), custom_call_target="tpu_custom_call" | custom-call | bytes 200000000 | tf_op jit(solution)/shard_map/pallas_call | solution.py:206
  93.2 9.1 %convolution_convert_fusion = bf16[4,624,512]{2,1,0:T(8,128)(2,1)S(1)} fusion(bf16[4,1664,624]{2,1,0:T(8,128)(2,1)} %bitcast.87, bf16[512,1664]{1,0:T(8,128)(2,1)S(1)} %copy-done, f32[1664]{0:T(1024)S(1)} %copy-done.11, f32[512]{0:T(512)S(1)} %add_rsqrt_fusion, f32[512]{0:T(512)S(1)} %broadcast_multiply_fusion), kind=kOutput, calls=%fused_computation.29 | convolution fusion | flops 4258562048 | bytes 12577280 | tf_op jit(solution)/shard_map/td,pdn->ptn/dot_general | solution.py:377
  102.3 0.9 slice.95
  103.2 0.8 fusion.27
  104.0 2.2 %fusion.42 = (f32[4,2,256]{2,1,0:T(2,128)S(1)}, f32[4,2,256,512]{3,2,1,0:T(8,128)S(1)}) fusion(f32[4,2,256,512]{3,2,1,0:T(8,128)S(1)} %fusion.27, pred[256,512]{1,0:T(8,128)(4,1)S(1)} %get-tuple-element.18), kind=kOutput, calls=%fused_computation.88 | output fusion | flops 6291967 | bytes 8527872 | tf_op jit(solution)/shard_map/sub | solution.py:360
  106.2 0.9 fusion.25
  107.1 1.0 copy-done.9
  108.1 1.3 fusion.43
  109.5 0.7 reduce_sum.113
  110.2 0.9 reduce_sum.114
  111.1 0.5 copy-done.6
  111.6 0.7 sub.67
  112.3 0.9 sub.68
  113.1 1.4 reshape.190
  114.6 0.3 multiply_reduce_fusion.1
  115.1 2.7 %select_convert_fusion.1.refs_0_ = bf16[64,6656]{1,0:T(8,128)(2,1)} fusion(f32[64,6656]{1,0:T(8,128)} %reshape.190, f32[6656]{0:T(1024)} %param.12, f32[64]{0:T(128)S(1)} %add_rsqrt_fusion.2, f32[64]{0:T(128)} %copy-done.6, pred[64]{0:T(512)(128)(4,1)} %get-tuple-element.14), kind=kLoop, calls=%fused_computation.33 | loop fusion | flops 2129920 | bytes 2583104 | tf_op jit(solution)/shard_map/convert_element_type | solution.py:393
  117.9 1.5 collective-permute-start.1
  119.4 2.0 %fusion.26 = f32[4,2,256,512]{3,2,1,0:T(8,128)S(1)} fusion(bf16[4,256,2,104]{1,3,2,0:T(8,128)(2,1)} %slice.95, bf16[4,512,3,2,104]{1,4,3,2,0:T(8,128)(2,1)} %bitcast.78), kind=kOutput, calls=%fused_computation.43 | convolution fusion | flops 218103808 | bytes 5472256 | tf_op jit(solution)/shard_map/pqhe,pkhe->phqk/dot_general | solution.py:356
  121.4 2.2 %fusion.44 = (f32[4,2,256]{2,1,0:T(2,128)S(1)}, f32[4,2,256,512]{3,2,1,0:T(8,128)S(1)}) fusion(f32[4,2,256,512]{3,2,1,0:T(8,128)S(1)} %fusion.26, pred[256,512]{1,0:T(8,128)(4,1)S(1)} %get-tuple-element.17), kind=kOutput, calls=%fused_computation.90 | output fusion | flops 6291967 | bytes 8527872 | tf_op jit(solution)/shard_map/sub | solution.py:360
  123.6 2.5 %fusion.24 = bf16[4,2,104,256]{3,2,1,0:T(8,128)(2,1)S(1)} fusion(f32[4,2,256,512]{3,2,1,0:T(8,128)S(1)} %get-tuple-element.28, f32[4,2,256]{2,1,0:T(2,128)S(1)} %get-tuple-element.27, bf16[4,512,3,2,104]{1,4,3,2,0:T(8,128)(2,1)} %bitcast.79), kind=kOutput, calls=%fused_computation.38 | convolution fusion | flops 220413952 | bytes 5480448 | tf_op jit(solution)/shard_map/phqk,pkhe->pqhe/dot_general | solution.py:362
  126.1 0.2 copy-done.10
  126.3 1.3 fusion.45
  128.0 0.1 sub.76
  128.1 0.3 reshape.192
  128.4 0.3 multiply_reduce_fusion
  128.9 0.3 select_convert_fusion.refs_1_
  129.3 0.5 collective-permute-start.2
  129.8 0.8 fusion.28.refs_5_
  130.5 27.1 %collective-permute-done.2.refs_3_ = bf16[64,6656]{1,0:T(8,128)(2,1)S(1)} collective-permute-done((bf16[64,6656]{1,0:T(8,128)(2,1)S(1)}, bf16[64,6656]{1,0:T(8,128)(2,1)S(1)}, u32[]{:S(2)}, u32[]{:S(2)}) %collective-permute-start.2) | collective-permute-done | bytes 852000 | tf_op jit(solution)/shard_map/ppermute | solution.py:394
  157.7 0.9 copy-done.3
  158.5 35.1 %shard_map.83 = bf16[512,1024]{1,0:T(8,128)(2,1)} custom-call(bf16[64,6656]{1,0:T(8,128)(2,1)} %select_convert_fusion.1.refs_0_, bf16[64,6656]{1,0:T(8,128)(2,1)} %copy-done.1, bf16[64,6656]{1,0:T(8,128)(2,1)} %collective-permute-done.1.refs_2_, bf16[64,6656]{1,0:T(8,128)(2,1)} %copy-done.3, bf16[6656,1024]{1,0:T(8,128)(2,1)} %all-gather.2.cloned.1.call-done.refs_4_, ...), custom_call_target="tpu_custom_call" | custom-call | flops 3489660928 | bytes 13631488 | tf_op jit(solution)/shard_map/pallas_call | solution.py:312
  193.6 2.3 %copy.45 = bf16[512,1024]{1,0:T(8,128)(2,1)} copy(bf16[512,1024]{1,0:T(8,128)(2,1)} %shard_map.83) | data formatting | bytes 2097152
  (49 shorter events, 1.2 us)
Async XLA Ops:
  6.5 4.5 %copy-start.8 = (s32[1024]{0:T(1024)S(1)}, s32[1024]{0:T(1024)}, u32[]{:S(2)}) copy-start(s32[1024]{0:T(1024)} %param.14) | copy-start | bytes 12292
  6.5 4.7 %copy-start.5 = (s32[256,1]{0,1:T(1,128)S(1)}, s32[256,1]{0,1:T(1,128)}, u32[]{:S(2)}) copy-start(s32[256,1]{0,1:T(1,128)} %param.15) | copy-start | bytes 3076
  6.5 6.3 %copy-start = (bf16[512,1664]{1,0:T(8,128)(2,1)S(1)}, bf16[512,1664]{1,0:T(8,128)(2,1)}, u32[]{:S(2)}) copy-start(bf16[512,1664]{1,0:T(8,128)(2,1)} %param.8) | copy-start | bytes 5111812
  6.5 151.1 %all-gather.2.cloned.1.call-start = ((), (), s32[]{:S(2)}) async-start(), calls=%async_computation | async-start | bytes 14483456 | tf_op jit(solution)/shard_map/all_gather | solution.py:371
  10.4 82.8 %copy-start.11 = (f32[1664]{0:T(1024)S(1)}, f32[1664]{0:T(1024)}, u32[]{:S(2)}) copy-start(f32[1664]{0:T(1024)} %param.9) | copy-start | bytes 19972
  10.5 3.5 %collective-permute-start = (bf16[104,832]{1,0:T(8,128)(2,1)S(1)}, bf16[104,832]{1,0:T(8,128)(2,1)S(1)}, u32[]{:S(2)}, u32[]{:S(2)}) collective-permute-start(bf16[104,832]{1,0:T(8,128)(2,1)S(1)} %select_bitcast_fusion), channel_id=1, source_target_pairs={{0,2},{2,0},{4,6},{6,4},{8,10},{10,8},{12,14},{14,12},{16,18},{18,... | collective-permute-start | bytes 519176 | tf_op jit(solution)/shard_map/ppermute | solution.py:346
  102.3 4.9 %copy-start.2 = (bf16[4,624,512]{2,1,0:T(8,128)(2,1)}, bf16[4,624,512]{2,1,0:T(8,128)(2,1)S(1)}, u32[]{:S(2)}) copy-start(bf16[4,624,512]{2,1,0:T(8,128)(2,1)S(1)} %convolution_convert_fusion) | copy-start | bytes 7667716
  106.2 2.0 copy-start.9
  111.1 0.5 copy-start.6
  117.9 39.8 %collective-permute-start.1 = (bf16[64,6656]{1,0:T(8,128)(2,1)}, bf16[64,6656]{1,0:T(8,128)(2,1)}, u32[]{:S(2)}, u32[]{:S(2)}) collective-permute-start(bf16[64,6656]{1,0:T(8,128)(2,1)} %select_convert_fusion.1.refs_0_), channel_id=1, source_target_pairs={{0,1},{1,0},{2,3},{3,2},{4,5},{5,4},{6,7},{7,6},{8,9},{9,8},{10,11... | collective-permute-start | bytes 2555912 | tf_op jit(solution)/shard_map/ppermute | solution.py:394
  123.6 2.7 %copy-start.10 = (bf16[4,8,208,208]{3,2,1,0:T(8,128)(2,1)S(1)}, bf16[4,8,208,208]{3,2,1,0:T(8,128)(2,1)}, u32[]{:S(2)}) copy-start(bf16[4,8,208,208]{3,2,1,0:T(8,128)(2,1)} %get-tuple-element.10) | copy-start | bytes 8306692
  127.7 1.3 copy-start.4
  127.7 1.3 copy-start.7
  129.3 28.4 %copy-start.1 = (bf16[64,6656]{1,0:T(8,128)(2,1)}, bf16[64,6656]{1,0:T(8,128)(2,1)S(1)}, u32[]{:S(2)}) copy-start(bf16[64,6656]{1,0:T(8,128)(2,1)S(1)} %select_convert_fusion.refs_1_) | copy-start | bytes 2555908
  129.3 28.4 %collective-permute-start.2 = (bf16[64,6656]{1,0:T(8,128)(2,1)S(1)}, bf16[64,6656]{1,0:T(8,128)(2,1)S(1)}, u32[]{:S(2)}, u32[]{:S(2)}) collective-permute-start(bf16[64,6656]{1,0:T(8,128)(2,1)S(1)} %select_convert_fusion.refs_1_), channel_id=1, source_target_pairs={{0,1},{1,0},{2,3},{3,2},{4,5},{5,4},{6,7},{7,6},{8,9},{9,8},{10,11... | collective-permute-start | bytes 2555912 | tf_op jit(solution)/shard_map/ppermute | solution.py:394
  157.6 0.9 copy-start.3
Sparse Core Ops, SparseCore 0:
  9.7 137.5 all-gather.1
